TPU v7x, 128 devices: a whole 4x4x4 slice. The times are simulated.
128 devices in a mesh: blk: 8 (over z, core), leaf: 16 (over x, y).
Axes of the slice: x: 4, y: 4, z: 4, core: 2. Of those that a mesh axis runs over, the one named last changes fastest.
Arguments:
- modes: float32 [32768, 3, 256], P(('blk', 'leaf')), may hold values from -60 to 60
- stiffness: float32 [10, 3, 10, 3, 16384], P(None, None, None, None, ('blk', 'leaf')), may hold values from -0.5 to 3.5, as said below
- connect: int32 [10, 16384], P(None, ('blk', 'leaf')), may hold values from 0 to 767
- send_list: int32 [128, 4, 128], P(('blk', 'leaf')), may hold values from 0 to 255
- elem_count: int32 [128], P(('blk', 'leaf')), may hold values from 64 to 128, as said below
Outputs:
- q_panel: float32 [32768, 3, 512], P(('blk', 'leaf'))
- r_factor: float32 [512, 512], replicated
Inputs may be any that keep to these rules, and one draw needn't show every extreme that they name: `elem_count`: the largest count equals 128. `stiffness`: symmetric under exchanging (k, c) with (l, c2).
All inputs are finite; a program needn't handle non-finite values.
Results may differ from a plain program's by a relative error of at most 0.0003.
Values sent between devices are 32-bit elements; how exact they have to be, the bound alone decides.
A program may use at most 128 MiB of HBM per device.

v0:
```python
import jax
import jax.numpy as jnp
from jax import lax
from jax.sharding import PartitionSpec as P


def from_behind(value, axis, steps):
    count = lax.axis_size(axis)
    initial, last = (max(0, -steps), min(count, count - steps))
    return lax.ppermute(value, axis, [(source, source + steps) for source in range(initial, last)])


def direction_offset(index, half):
    return index - half + (1 if index >= half else 0)


def shards(modes, stiffness, connect, send_list, elem_count):
    own_nodes = modes.shape[0]
    direction_total = send_list.shape[1]
    half = direction_total // 2
    slot_most = send_list.shape[2]
    element_total = connect.shape[1]
    send_table = send_list[0]
    arrivals = []
    for j in range(direction_total):
        outgoing = modes[send_table[j]]
        arrivals.append(from_behind(outgoing, ("blk", "leaf"), direction_offset(j, half)))
    extended = jnp.concatenate([modes] + arrivals, axis=0)
    block_size = min(256, element_total)
    live_count = elem_count[0]

    def element_block(step, accumulated):
        start = step * block_size
        blocks = stiffness
        positions = start + jnp.arange(block_size, dtype=jnp.int32)
        blocks = jnp.where(positions < live_count, blocks, 0.0)
        gathered = extended[connect]
        product = jnp.einsum("kcldE,lEdm->kEcm", blocks, gathered, precision=lax.Precision.HIGHEST)
        return accumulated.at[connect].add(product)

    accumulated = jnp.zeros(extended.shape, jnp.float32)
    trips = element_total // block_size
    accumulated = lax.fori_loop(0, trips, element_block, accumulated)
    stiff_modes = accumulated[:own_nodes]
    for j in range(direction_total):
        returned = accumulated[own_nodes + j * slot_most : own_nodes + (j + 1) * slot_most]
        incoming = from_behind(returned, ("blk", "leaf"), -direction_offset(j, half))
        stiff_modes = stiff_modes.at[send_table[j]].add(incoming)
    panel = jnp.concatenate([modes, stiff_modes], axis=2)
    columns = panel.shape[2]
    flat = panel.reshape(-1, columns)
    local_gram = jnp.einsum("rc,rd->cd", flat, flat, precision=lax.Precision.HIGHEST)
    total_gram = lax.psum(local_gram, ("blk", "leaf"))
    lower = jnp.linalg.cholesky(total_gram)
    row_total = 3 * own_nodes * lax.axis_size("blk") * lax.axis_size("leaf")
    scale = jnp.sqrt(jnp.float32(row_total))
    solved = jax.scipy.linalg.solve_triangular(lower, flat.T, lower=True).T
    q_panel = (solved * scale).reshape(own_nodes, 3, columns)
    r_factor = lower.T / scale
    return (q_panel, r_factor)


def solution(mesh):
    placed = (
        P(("blk", "leaf"), None, None),
        P(None, None, None, None, ("blk", "leaf")),
        P(None, ("blk", "leaf")),
        P(("blk", "leaf"), None, None),
        P(("blk", "leaf")),
    )
    return jax.shard_map(
        shards,
        mesh=mesh,
        in_specs=placed,
        out_specs=(P(("blk", "leaf"), None, None), P()),
        check_vma=False,
    )
```

profile of v0, /device:TPU:0, one launch (start us, length us, event | category | flops | bytes accessed | tf_op | source)
XLA Modules:
  0.0 601.8 jit_solution(17781172038513062521)
XLA Ops:
  17.6 5.3 collective-permute-start.2
  24.9 6.5 %collective-permute-start.3 = (f32[128,3,256]{2,0,1:T(8,128)}, f32[128,3,256]{2,0,1:T(8,128)}, u32[]{:S(2)}, u32[]{:S(2)}) collective-permute-start(f32[128,3,256]{2,0,1:T(8,128)} %gather_fusion.3), channel_id=1, source_target_pairs={{0,2},{1,3},{2,4},{3,5},{4,6},{5,7},{6,8},{7,9},{8,10},{9,11},{10,... | collective-permute-start | bytes 1179656 | tf_op jit(solution)/shard_map/ppermute | solution.py:10
  34.6 7.1 %copy.20 = f32[10,3,10,3,128]{2,0,3,1,4:T(8,128)} copy(f32[10,3,10,3,128]{4,3,2,1,0:T(4,128)} %broadcast_select_fusion) | data formatting | bytes 921600 | tf_op jit(solution)/shard_map/while/body/eval_jaxpr/jit(_where)/select_n | solution.py:36
  47.0 6.1 %gather_fusion.4 = f32[1280,3,256]{2,1,0:T(4,128)} fusion(f32[768,3,256]{2,1,0:T(4,128)S(1)} %copy_dynamic-update-slice_fusion.2, s32[2048]{0:T(1024)S(1)} %pad_clamp_fusion), kind=kCustom, calls=%fused_computation.4 | custom fusion | bytes 7869440 | tf_op jit(solution)/shard_map/while/body/eval_jaxpr/gather | solution.py:37
  53.1 14.4 %fusion.2 = f32[10,128,3,256]{3,0,2,1:T(8,128)S(1)} fusion(f32[10,3,10,3,128]{2,0,3,1,4:T(8,128)} %copy.20, f32[10,128,3,256,1]{3,2,1,0,4:T(4,128)} %bitcast.87), kind=kOutput, calls=%fused_computation.14 | convolution fusion | flops 353894400 | bytes 8325120 | tf_op jit(solution)/shard_map/while/body/eval_jaxpr/kcldE,lEdm->kEcm/dot_general | solution.py:38
  69.8 10.7 %copy.22 = f32[1280,3,256]{2,1,0:T(4,128)} copy(f32[1280,3,256]{2,0,1:T(8,128)S(1)} %bitcast.88) | data formatting | bytes 7864320 | tf_op jit(solution)/shard_map/while/body/eval_jaxpr/kcldE,lEdm->kEcm/transpose | solution.py:38
  80.9 94.6 %scatter_fusion = f32[768,3,256]{2,1,0:T(4,128)S(1)} fusion(f32[768,3,256]{2,1,0:T(4,128)S(1)} %broadcast_in_dim.28, s32[1280]{0:T(1024)S(1)} %fusion.35, f32[1280,3,256]{2,1,0:T(4,128)} %copy.22), kind=kCustom, calls=%fused_computation.5 | custom fusion | flops 983040 | bytes 11801600 | tf_op jit(solution)/shard_map/while/body/eval_jaxpr/scatter-add | solution.py:39
  176.9 6.0 collective-permute-start.4
  182.9 3.4 collective-permute-start.5
  194.0 15.6 %scatter_fusion.1 = f32[256,3,256]{2,1,0:T(4,128)} fusion(f32[256,3,256]{2,1,0:T(4,128)} %slice.179, s32[128]{0:T(128)S(1)} %copy-done.15, f32[128,3,256]{2,1,0:T(4,128)} %collective-permute-done.4), kind=kCustom, calls=%fused_computation.6 | custom fusion | flops 98304 | bytes 1180160 | tf_op jit(solution)/shard_map/scatter-add | solution.py:48
  209.7 15.6 %scatter_fusion.2 = f32[256,3,256]{2,1,0:T(4,128)} fusion(f32[256,3,256]{2,1,0:T(4,128)} %scatter_fusion.1, s32[128]{0:T(128)S(1)} %copy-done.13, f32[128,3,256]{2,1,0:T(4,128)} %collective-permute-done.5), kind=kCustom, calls=%fused_computation.7 | custom fusion | flops 98304 | bytes 1180160 | tf_op jit(solution)/shard_map/scatter-add | solution.py:48
  226.6 15.6 %scatter_fusion.3 = f32[256,3,256]{2,1,0:T(4,128)} fusion(f32[256,3,256]{2,1,0:T(4,128)} %scatter_fusion.2, s32[128]{0:T(128)S(1)} %copy-done.11, f32[128,3,256]{2,1,0:T(4,128)} %collective-permute-done.6), kind=kCustom, calls=%fused_computation.8 | custom fusion | flops 98304 | bytes 1180160 | tf_op jit(solution)/shard_map/scatter-add | solution.py:48
  242.2 15.6 %scatter_fusion.4 = f32[256,3,256]{2,1,0:T(4,128)} fusion(f32[256,3,256]{2,1,0:T(4,128)} %scatter_fusion.3, s32[128]{0:T(128)S(1)} %copy-done.9, f32[128,3,256]{2,1,0:T(4,128)} %collective-permute-done.7), kind=kCustom, calls=%fused_computation.9 | custom fusion | flops 98304 | bytes 1180160 | tf_op jit(solution)/shard_map/scatter-add | solution.py:48
  259.1 3.7 convolution_bitcast_fusion
  268.2 166.1 %all-reduce.3.cloned.1.call-done = f32[512,512]{0,1:T(8,128)} async-done(((f32[512,512]{0,1:T(8,128)}), f32[512,512]{0,1:T(8,128)}) %all-reduce.3.cloned.1.call-update) | async-done | bytes 1048592 | tf_op jit(solution)/shard_map/psum | solution.py:53
  438.3 11.7 %cholesky.106 = f32[128,128]{1,0:T(8,128)S(1)} custom-call(f32[128,128]{1,0:T(8,128)S(1)} %cholesky.269), custom_call_target="Cholesky" | custom-call | tf_op jit(solution)/shard_map/jit(cholesky)/cholesky | solution.py:54
  450.1 9.8 %custom-call.31 = f32[1,128,128]{1,2,0:T(8,128)S(1)} custom-call(f32[1,128,128]{2,1,0:T(8,128)S(1)} %get-tuple-element.60), custom_call_target="InvertDiagBlocksLowerTriangular" | custom-call | tf_op jit(solution)/shard_map/jit(cholesky)/cholesky | solution.py:54
  462.5 11.7 %cholesky.220 = f32[128,128]{1,0:T(8,128)S(1)} custom-call(f32[128,128]{1,0:T(8,128)S(1)} %cholesky.273), custom_call_target="Cholesky" | custom-call | tf_op jit(solution)/shard_map/jit(cholesky)/cholesky | solution.py:54
  474.2 10.0 %custom-call.32 = f32[1,128,128]{1,2,0:T(8,128)S(1)} custom-call(f32[1,128,128]{2,1,0:T(8,128)S(1)} %get-tuple-element.57), custom_call_target="InvertDiagBlocksLowerTriangular" | custom-call | tf_op jit(solution)/shard_map/jit(cholesky)/cholesky | solution.py:54
  485.8 11.7 %cholesky.241 = f32[128,128]{1,0:T(8,128)S(1)} custom-call(f32[128,128]{1,0:T(8,128)S(1)} %cholesky.278), custom_call_target="Cholesky" | custom-call | tf_op jit(solution)/shard_map/jit(cholesky)/cholesky | solution.py:54
  498.3 9.8 %custom-call.33 = f32[1,128,128]{1,2,0:T(8,128)S(1)} custom-call(f32[1,128,128]{2,1,0:T(8,128)S(1)} %get-tuple-element.54), custom_call_target="InvertDiagBlocksLowerTriangular" | custom-call | tf_op jit(solution)/shard_map/jit(cholesky)/cholesky | solution.py:54
  509.6 11.7 %cholesky.258 = f32[128,128]{1,0:T(8,128)S(1)} custom-call(f32[128,128]{1,0:T(8,128)S(1)} %convolution_subtract_fusion.5), custom_call_target="Cholesky" | custom-call | tf_op jit(solution)/shard_map/jit(cholesky)/cholesky | solution.py:54
  527.0 11.7 %while.1 = (s32[]{:T(128)}, f32[512,512]{1,0:T(8,128)}, s32[4,2]{0,1:T(2,128)S(1)}, f32[4,128,128]{2,1,0:T(8,128)S(1)}, s32[]{:T(128)}) while((s32[]{:T(128)}, f32[512,512]{1,0:T(8,128)}, s32[4,2]{0,1:T(2,128)S(1)}, f32[4,128,128]{2,1,0:T(8,128)S(1)}, s32[]{:T(128)}) %tuple.42), condition=%wide.while_cond, body=%wide.while_body.sunk | while | flops 2 | bytes 131181 | solution.py:57
  538.7 39.3 %custom-call.34 = f32[4,128,128]{1,2,0:T(8,128)S(1)} custom-call(f32[4,128,128]{2,1,0:T(8,128)S(1)} %get-tuple-element.30), custom_call_target="InvertDiagBlocksLowerTriangular" | custom-call | tf_op jit(solution)/shard_map/jit(_solve_triangular)/triangular_solve | solution.py:57
  (119 shorter events, 81.3 us)
Async XLA Ops:
  7.2 5.2 copy-start
  7.2 427.1 %all-reduce.3.cloned.1.call-start = ((), (), s32[]{:S(2)}) async-start(), calls=%async_computation | async-start | bytes 2097152 | tf_op jit(solution)/shard_map/psum | solution.py:53
  8.1 6.3 %copy-start.12 = (s32[128]{0:T(128)}, s32[128]{0:T(128)S(1)}, u32[]{:S(2)}) copy-start(s32[128]{0:T(128)S(1)} %get-tuple-element.62) | copy-start | bytes 1540
  8.1 7.6 %copy-start.10 = (s32[128]{0:T(128)}, s32[128]{0:T(128)S(1)}, u32[]{:S(2)}) copy-start(s32[128]{0:T(128)S(1)} %get-tuple-element.64) | copy-start | bytes 1540
  8.1 14.9 %copy-start.8 = (s32[128]{0:T(128)}, s32[128]{0:T(128)S(1)}, u32[]{:S(2)}) copy-start(s32[128]{0:T(128)S(1)} %get-tuple-element.61) | copy-start | bytes 1540
  11.1 30.6 %collective-permute-start = (f32[128,3,256]{2,0,1:T(8,128)S(1)}, f32[128,3,256]{2,0,1:T(8,128)}, u32[]{:S(2)}, u32[]{:S(2)}) collective-permute-start(f32[128,3,256]{2,0,1:T(8,128)S(1)} %gather_fusion), channel_id=1, source_target_pairs={{2,0},{3,1},{4,2},{5,3},{6,4},{7,5},{8,6},{9,7},{10,8},{11,9},{12,... | collective-permute-start | bytes 1179656 | tf_op jit(solution)/shard_map/ppermute | solution.py:10
  14.4 28.7 %collective-permute-start.1 = (f32[128,3,256]{2,0,1:T(8,128)}, f32[128,3,256]{2,0,1:T(8,128)}, u32[]{:S(2)}, u32[]{:S(2)}) collective-permute-start(f32[128,3,256]{2,0,1:T(8,128)} %gather_fusion.1), channel_id=1, source_target_pairs={{1,0},{2,1},{3,2},{4,3},{5,4},{6,5},{7,6},{8,7},{9,8},{10,9},{11,1... | collective-permute-start | bytes 1179656 | tf_op jit(solution)/shard_map/ppermute | solution.py:10
  17.6 26.7 %collective-permute-start.2 = (f32[128,3,256]{2,0,1:T(8,128)}, f32[128,3,256]{2,0,1:T(8,128)}, u32[]{:S(2)}, u32[]{:S(2)}) collective-permute-start(f32[128,3,256]{2,0,1:T(8,128)} %gather_fusion.2), channel_id=1, source_target_pairs={{0,1},{1,2},{2,3},{3,4},{4,5},{5,6},{6,7},{7,8},{8,9},{9,10},{10,1... | collective-permute-start | bytes 1179656 | tf_op jit(solution)/shard_map/ppermute | solution.py:10
  22.9 10.7 %copy-start.6 = (f32[10,3,10,3,128]{4,3,2,1,0:T(4,128)S(1)}, f32[10,3,10,3,128]{4,3,2,1,0:T(4,128)}, u32[]{:S(2)}) copy-start(f32[10,3,10,3,128]{4,3,2,1,0:T(4,128)} %param.6) | copy-start | bytes 1382404
  22.9 11.6 %copy-start.7 = (s32[10,128]{1,0:T(8,128)S(1)}, s32[10,128]{1,0:T(8,128)}, u32[]{:S(2)}) copy-start(s32[10,128]{1,0:T(8,128)} %param.7) | copy-start | bytes 15364
  24.9 20.8 %collective-permute-start.3 = (f32[128,3,256]{2,0,1:T(8,128)}, f32[128,3,256]{2,0,1:T(8,128)}, u32[]{:S(2)}, u32[]{:S(2)}) collective-permute-start(f32[128,3,256]{2,0,1:T(8,128)} %gather_fusion.3), channel_id=1, source_target_pairs={{0,2},{1,3},{2,4},{3,5},{4,6},{5,7},{6,8},{7,9},{8,10},{9,11},{10,... | collective-permute-start | bytes 1179656 | tf_op jit(solution)/shard_map/ppermute | solution.py:10
  34.6 7.2 %copy-start.3 = (f32[768,3,256]{2,1,0:T(4,128)S(1)}, f32[768,3,256]{2,1,0:T(4,128)}, u32[]{:S(2)}) copy-start(f32[768,3,256]{2,1,0:T(4,128)} %copy_dynamic-update-slice_fusion) | copy-start | bytes 7077892
  175.6 13.4 %copy-start.1 = (f32[256,3,256]{2,0,1:T(8,128)S(1)}, f32[256,3,256]{2,0,1:T(8,128)}, u32[]{:S(2)}) copy-start(f32[256,3,256]{2,0,1:T(8,128)} %param.5) | copy-start | bytes 2359300
  175.6 18.5 %copy-start.15 = (s32[128]{0:T(128)S(1)}, s32[128]{0:T(128)}, u32[]{:S(2)}) copy-start(s32[128]{0:T(128)} %copy-done.14) | copy-start | bytes 1540
  176.9 32.7 %copy-start.13 = (s32[128]{0:T(128)S(1)}, s32[128]{0:T(128)}, u32[]{:S(2)}) copy-start(s32[128]{0:T(128)} %copy-done.12) | copy-start | bytes 1540
  176.9 17.1 %collective-permute-start.4 = (f32[128,3,256]{2,1,0:T(4,128)S(1)}, f32[128,3,256]{2,1,0:T(4,128)}, u32[]{:S(2)}, u32[]{:S(2)}) collective-permute-start(f32[128,3,256]{2,1,0:T(4,128)S(1)} %get-tuple-element.48), channel_id=1, source_target_pairs={{0,2},{1,3},{2,4},{3,5},{4,6},{5,7},{6,8},{7,9},{8,10},{9,11},{10,... | collective-permute-start | bytes 1179656 | tf_op jit(solution)/shard_map/ppermute | solution.py:10
  182.9 26.7 %collective-permute-start.5 = (f32[128,3,256]{2,1,0:T(4,128)}, f32[128,3,256]{2,1,0:T(4,128)}, u32[]{:S(2)}, u32[]{:S(2)}) collective-permute-start(f32[128,3,256]{2,1,0:T(4,128)} %get-tuple-element.47), channel_id=1, source_target_pairs={{0,1},{1,2},{2,3},{3,4},{4,5},{5,6},{6,7},{7,8},{8,9},{9,10},{10,1... | collective-permute-start | bytes 1179656 | tf_op jit(solution)/shard_map/ppermute | solution.py:10
  186.3 40.2 %collective-permute-start.6 = (f32[128,3,256]{2,1,0:T(4,128)}, f32[128,3,256]{2,1,0:T(4,128)}, u32[]{:S(2)}, u32[]{:S(2)}) collective-permute-start(f32[128,3,256]{2,1,0:T(4,128)} %get-tuple-element.46), channel_id=1, source_target_pairs={{1,0},{2,1},{3,2},{4,3},{5,4},{6,5},{7,6},{8,7},{9,8},{10,9},{11,1... | collective-permute-start | bytes 1179656 | tf_op jit(solution)/shard_map/ppermute | solution.py:10
  187.6 38.9 %copy-start.11 = (s32[128]{0:T(128)S(1)}, s32[128]{0:T(128)}, u32[]{:S(2)}) copy-start(s32[128]{0:T(128)} %copy-done.10) | copy-start | bytes 1540
  187.6 54.5 %collective-permute-start.7 = (f32[128,3,256]{2,1,0:T(4,128)}, f32[128,3,256]{2,1,0:T(4,128)}, u32[]{:S(2)}, u32[]{:S(2)}) collective-permute-start(f32[128,3,256]{2,1,0:T(4,128)} %get-tuple-element.45), channel_id=1, source_target_pairs={{2,0},{3,1},{4,2},{5,3},{6,4},{7,5},{8,6},{9,7},{10,8},{11,9},{12,... | collective-permute-start | bytes 1179656 | tf_op jit(solution)/shard_map/ppermute | solution.py:10
  189.9 52.3 %copy-start.9 = (s32[128]{0:T(128)S(1)}, s32[128]{0:T(128)}, u32[]{:S(2)}) copy-start(s32[128]{0:T(128)} %copy-done.8) | copy-start | bytes 1540
  191.0 66.8 %copy-start.2 = (f32[256,3,512]{2,0,1:T(8,128)S(1)}, f32[256,3,512]{2,0,1:T(8,128)}, u32[]{:S(2)}) copy-start(f32[256,3,512]{2,0,1:T(8,128)} %constant_dynamic-update-slice_fusion) | copy-start | bytes 4718596
  437.3 1.0 copy-start.5
  588.9 4.3 copy-start.4
  (1 other events, 0.6 us)
Sparse Core Ops, SparseCore 0:
  263.0 171.2 all-reduce.2
where the time goes:
time: 613 us; the launch traced here: 602 us
  other arithmetic  280 us (46%)
  waiting for transfers between devices  170 us (28%)
  local copies, waits for them, and re-layouts  73.8 us (12%)
  matrix products  32.7 us (5%)
  starting transfers between devices  26.4 us (4%)
  between operations  18.2 us (3%)
    psum x1, waiting for transfers between devices, shards(): total_gram = lax.psum(local_gram, ('blk', 'leaf'))  166 us
    scatter-add x1, other arithmetic, element_block(): return accumulated.at[connect].add(product)  94.6 us
    another operation x14, other arithmetic, shards(): lower = jnp.linalg.cholesky(total_gram)  78.6 us
    scatter-add x4, other arithmetic, shards(): stiff_modes = stiff_modes.at[send_table[j]].add(incoming)  62.4 us
    another operation x2, other arithmetic, shards(): solved = jax.scipy.linalg.solve_triangular(lower, flat.T, lower=True).T  39.3 us
    ppermute x8, starting transfers between devices, from_behind(): lax.ppermute(value, axis, [(source, source + steps) for source in range(i...  26.4 us
    dot_general x1, matrix products, element_block(): jnp.einsum('kcldE,lEdm->kEcm', blocks, gathered, precision=lax.Precision....  14.4 us
    transpose x2, local copies, waits for them, and re-layouts, element_block(): jnp.einsum('kcldE,lEdm->kEcm', blocks, gathered, precision=lax.Precision....  12.9 us
  transfers between devices with their start and end apart: 9, of which 3 were waited for; matrix products, arithmetic and copies ran while one was open for 12% of the time, Pallas kernels for 0%

commit v1 on v0

v1 whole, which is shorter than its diff:
```python
import functools

import jax
import jax.numpy as jnp
from jax import lax
from jax.experimental import pallas as pl
from jax.experimental.pallas import tpu as pltpu
from jax.sharding import PartitionSpec as P

HIGH = lax.Precision.HIGHEST
F32 = jnp.float32
BF16 = jnp.bfloat16
MESH = pl.DeviceIdType.MESH
VMEM = pl.BlockSpec(memory_space=pltpu.VMEM)
SMEM = pl.BlockSpec(memory_space=pltpu.SMEM)
LIMIT = 56 * 1024 * 1024


def dot(a, b, ca, cb, precision=None):
    return lax.dot_general(a, b, (((ca,), (cb,)), ((), ())), precision=precision, preferred_element_type=F32)


def split2(x):
    hi = x.astype(BF16)
    return hi, (x - hi.astype(F32)).astype(BF16)


def split3(x):
    hi = x.astype(BF16)
    rest = x - hi.astype(F32)
    mid = rest.astype(BF16)
    return hi, mid, (rest - mid.astype(F32)).astype(BF16)


def columns_of(rows, count):
    padded = jnp.concatenate([rows.astype(F32), jnp.zeros((16 - count, 128), F32)], axis=0)
    return padded.T


N_LEAF = 16
N_BLK = 8
CHUNK = 24


def greet(leaf, blk):
    barrier = pltpu.get_barrier_semaphore()
    for k in range(1, N_LEAF):
        pl.semaphore_signal(barrier, inc=1, device_id={"leaf": lax.rem(leaf + k, N_LEAF)}, device_id_type=MESH)
    for k in range(1, N_BLK):
        pl.semaphore_signal(barrier, inc=1, device_id={"blk": lax.rem(blk + k, N_BLK)}, device_id_type=MESH)
    return barrier


class Sum:
    def __init__(self, leaf, blk, local, near, far, total, leaf_sems, blk_sems):
        self.leaf, self.blk = leaf, blk
        self.local, self.near, self.far, self.total = local, near, far, total
        mine = pl.ds(pl.multiple_of(leaf * CHUNK, 8), CHUNK)
        self.mine = mine
        self.spread, self.cross, self.collect = [], [], []
        for k in range(1, N_LEAF):
            peer = lax.rem(leaf + k, N_LEAF)
            self.spread.append(pltpu.make_async_remote_copy(
                src_ref=local.at[pl.ds(pl.multiple_of(peer * CHUNK, 8), CHUNK)], dst_ref=near.at[k],
                send_sem=leaf_sems.at[0, k], recv_sem=leaf_sems.at[1, k], device_id={"leaf": peer}, device_id_type=MESH))
            self.collect.append(pltpu.make_async_remote_copy(
                src_ref=total.at[mine], dst_ref=total.at[mine],
                send_sem=leaf_sems.at[2, k], recv_sem=leaf_sems.at[3, k], device_id={"leaf": peer}, device_id_type=MESH))
        for k in range(1, N_BLK):
            peer = lax.rem(blk + k, N_BLK)
            self.cross.append(pltpu.make_async_remote_copy(
                src_ref=far.at[blk], dst_ref=far.at[blk],
                send_sem=blk_sems.at[0, k], recv_sem=blk_sems.at[1, k], device_id={"blk": peer}, device_id_type=MESH))

    def begin(self, top, low, bottom):
        self.local[0:128, :] = top
        self.local[128:256, :] = low
        self.local[256:384, :] = bottom
        for copy in self.spread:
            copy.start()

    def across(self):
        part = self.local[self.mine, :]
        for k, copy in enumerate(self.spread):
            copy.wait_recv()
            part = part + self.near[k + 1]
        self.far[self.blk] = part
        for copy in self.cross:
            copy.start()

    def gather(self):
        for copy in self.cross:
            copy.wait_recv()
        part = self.far[0]
        for b in range(1, N_BLK):
            part = part + self.far[b]
        self.total[self.mine, :] = part
        for copy in self.collect:
            copy.start()

    def end(self):
        for copy in self.collect:
            copy.wait_recv()

    def drain(self):
        for copy in self.spread + self.cross + self.collect:
            copy.wait_send()


def sum_scratch():
    return [
        pltpu.VMEM((384, 128), F32),
        pltpu.VMEM((N_LEAF, CHUNK, 128), F32),
        pltpu.VMEM((N_BLK, CHUNK, 128), F32),
        pltpu.VMEM((384, 128), F32),
        pltpu.SemaphoreType.DMA((4, N_LEAF)),
        pltpu.SemaphoreType.DMA((2, N_BLK)),
    ]


class AxisSum:
    def __init__(self, leaf, blk, local, along_x, part, along_y, far, total, sems, blk_sems):
        self.blk, self.local, self.part, self.total = blk, local, part, total
        self.along_x, self.along_y, self.far = along_x, along_y, far
        x, y = lax.div(leaf, 4), lax.rem(leaf, 4)
        wide, slim = 4 * CHUNK, CHUNK
        self.wide = pl.ds(pl.multiple_of(x * wide, 8), wide)
        self.slim = pl.ds(pl.multiple_of(y * slim, 8), slim)
        self.mine = pl.ds(pl.multiple_of(leaf * slim, 8), slim)
        self.stages = [[], [], [], [], []]

        def copy(stage, k, src, dst, sem, peer):
            self.stages[stage].append(pltpu.make_async_remote_copy(
                src_ref=src, dst_ref=dst, send_sem=sem.at[0, k], recv_sem=sem.at[1, k],
                device_id=peer, device_id_type=MESH))

        for k in range(1, 4):
            px, py = lax.rem(x + k, 4), lax.rem(y + k, 4)
            beside, above = {"leaf": px * 4 + y}, {"leaf": x * 4 + py}
            copy(0, k, local.at[pl.ds(pl.multiple_of(px * wide, 8), wide)], along_x.at[k], sems.at[0], beside)
            copy(1, k, part.at[pl.ds(pl.multiple_of(py * slim, 8), slim)], along_y.at[k], sems.at[1], above)
            copy(3, k, total.at[self.mine], total.at[self.mine], sems.at[2], above)
            copy(4, k, total.at[self.wide], total.at[self.wide], sems.at[3], beside)
        for k in range(1, N_BLK):
            copy(2, k, far.at[blk], far.at[blk], blk_sems, {"blk": lax.rem(blk + k, N_BLK)})

    def start(self, stage):
        for copy in self.stages[stage]:
            copy.start()

    def wait(self, stage):
        for copy in self.stages[stage]:
            copy.wait_recv()

    def begin(self, top, low, bottom):
        self.local[0:128, :] = top
        self.local[128:256, :] = low
        self.local[256:384, :] = bottom
        self.start(0)

    def second(self):
        self.wait(0)
        part = self.local[self.wide, :]
        for k in range(1, 4):
            part = part + self.along_x[k]
        self.part[...] = part
        self.start(1)

    def third(self):
        self.wait(1)
        part = self.part[self.slim, :]
        for k in range(1, 4):
            part = part + self.along_y[k]
        self.far[self.blk] = part
        self.start(2)

    def fourth(self):
        self.wait(2)
        part = self.far[0]
        for b in range(1, N_BLK):
            part = part + self.far[b]
        self.total[self.mine, :] = part
        self.start(3)

    def fifth(self):
        self.wait(3)
        self.start(4)

    def end(self):
        self.wait(4)

    def drain(self):
        for stage in self.stages:
            for copy in stage:
                copy.wait_send()


def axis_sum_scratch():
    return [
        pltpu.VMEM((384, 128), F32),
        pltpu.VMEM((4, 4 * CHUNK, 128), F32),
        pltpu.VMEM((4 * CHUNK, 128), F32),
        pltpu.VMEM((4, CHUNK, 128), F32),
        pltpu.VMEM((N_BLK, CHUNK, 128), F32),
        pltpu.VMEM((384, 128), F32),
        pltpu.SemaphoreType.DMA((4, 2, 4)),
        pltpu.SemaphoreType.DMA((2, N_BLK)),
    ]


SIDE = 256
BLOCK = 64


def unpack(packed):
    top, low, bottom = packed[0:128, :], packed[128:256, :], packed[256:384, :]
    return jnp.concatenate([jnp.concatenate([top, low.T], axis=1), jnp.concatenate([low, bottom], axis=1)], axis=0)


def factor_start(work, gram):
    work[:, 0:SIDE] = gram
    work[:, SIDE:] = (
        lax.broadcasted_iota(jnp.int32, (SIDE, SIDE), 0) == lax.broadcasted_iota(jnp.int32, (SIDE, SIDE), 1)
    ).astype(F32)


def factor(work, first, last):
    sub = lax.broadcasted_iota(jnp.int32, (8, 128), 0)
    for start in range(first, last, BLOCK):
        left = start // 128 * 128
        right = SIDE + -(-(start + BLOCK) // 128) * 128
        if start:
            update = dot(work[0:start, start : start + BLOCK], work[0:start, left:right], 0, 0, HIGH)
            work[start : start + BLOCK, left:right] = work[start : start + BLOCK, left:right] - update
        tiles = (right - left) // 128
        count = BLOCK // 8
        x = [[work[start + 8 * t : start + 8 * t + 8, left + 128 * i : left + 128 * (i + 1)] for i in range(tiles)]
             for t in range(count)]
        for p in range(count):
            tile, lane = divmod(start + 8 * p - left, 128)
            rest = range(p, count)
            col = [{t: jnp.broadcast_to(x[t][tile][:, lane + j : lane + j + 1], (8, 128)) for t in rest} for j in range(8)]
            entry = {(i, k): jnp.broadcast_to(col[k][p][i : i + 1, :], (8, 128)) for k in range(8) for i in range(k, 8)}
            for j in range(8):
                inverse = lax.rsqrt(entry[j, j])
                scaled = {k: entry[k, j] * inverse for k in range(j + 1, 8)}
                low = {t: col[j][t] * inverse for t in rest}
                for k in range(j + 1, 8):
                    for i in range(k, 8):
                        entry[i, k] = entry[i, k] - scaled[i] * scaled[k]
                    for t in rest:
                        col[k][t] = col[k][t] - low[t] * scaled[k]
                for i in range(tiles):
                    row = jnp.broadcast_to(x[p][i][j : j + 1, :], (8, 128)) * inverse
                    for t in rest:
                        moved = x[t][i] - low[t] * row
                        if t == p:
                            moved = jnp.where(sub > j, moved, jnp.where(sub == j, row, x[t][i]))
                        x[t][i] = moved
            for i in range(tiles):
                work[start + 8 * p : start + 8 * p + 8, left + 128 * i : left + 128 * (i + 1)] = x[p][i]


def upper(x):
    keep = lax.broadcasted_iota(jnp.int32, (SIDE, SIDE), 0) <= lax.broadcasted_iota(jnp.int32, (SIDE, SIDE), 1)
    return jnp.where(keep, x, 0.0)


TOTAL = N_LEAF * N_BLK
STEPS = (-1, 1)


class Exchange:
    def __init__(self, device, near, far, relay, near_to, far_to, sems):
        self.near_to, self.far_to = near_to, far_to
        self.direct, self.away, self.onward = [], [], []
        self.one, self.two, self.from_one, self.from_two = [], [], [], []
        self.between = (device >= 1) & (device < TOTAL - 1)
        for u, step in enumerate(STEPS):
            peer = lax.rem(device + step + TOTAL, TOTAL)
            there = (lax.div(peer, N_LEAF), lax.rem(peer, N_LEAF))

            def copy(kind, src, dst):
                return pltpu.make_async_remote_copy(
                    src_ref=src, dst_ref=dst, send_sem=sems.at[0, kind, u], recv_sem=sems.at[1, kind, u],
                    device_id=there, device_id_type=MESH)

            self.direct.append(copy(0, near[u], near_to[u]))
            self.away.append(copy(1, far[u], relay.at[u]))
            self.onward.append(copy(2, relay.at[u], far_to[u]))
            self.one.append(self.within(device + step))
            self.two.append(self.within(device + 2 * step))
            self.from_one.append(self.within(device - step))
            self.from_two.append(self.within(device - 2 * step))

    def within(self, device):
        return (device >= 0) & (device < TOTAL)

    def send_far(self):
        for u in range(2):
            pl.when(self.two[u])(self.away[u].start)

    def send_near(self):
        for u in range(2):
            pl.when(self.one[u])(self.direct[u].start)

    def forward(self):
        for u in range(2):
            @pl.when(self.between)
            def _():
                self.away[u].wait_recv()
                self.onward[u].start()

    def receive(self, arrives, copy, to):
        pl.when(arrives)(copy.wait_recv)

        @pl.when(jnp.logical_not(arrives))
        def _():
            to[...] = jnp.zeros(to.shape, F32)

    def receive_near(self):
        for u in range(2):
            self.receive(self.from_one[u], self.direct[u], self.near_to[u])

    def receive_far(self):
        for u in range(2):
            self.receive(self.from_two[u], self.onward[u], self.far_to[u])

    def drain(self):
        for u in range(2):
            pl.when(self.two[u])(self.away[u].wait_send)
            pl.when(self.one[u])(self.direct[u].wait_send)
            pl.when(self.between)(self.onward[u].wait_send)


STORED = (512, 256, 384, 640)
NEAR_OUT, FAR_OUT = (1, 2), (0, 3)
NEAR_BACK, FAR_BACK = (2, 1), (3, 0)


def main_kernel(count, modes, stiffness, connect, send, g22_out, low_out, rest_out, r_out, q_out,
                outgoing, table, relay, acc, incoming, relay_back, halo_sems, back_sems,
                ext_hi, ext_lo, pick, place, taken, blocks, matrix_hi, matrix_lo, product, stiff, work, *sums):
    leaf, blk = lax.axis_index("leaf"), lax.axis_index("blk")
    device = blk * N_LEAF + leaf
    barrier = greet(leaf, blk)

    def rows_of(ref, h, j):
        return ref.at[h, pl.ds(STORED[j], 128)]

    halo, back = [], []
    for h in range(2):
        halo.append(Exchange(
            device, [outgoing.at[h, j] for j in NEAR_OUT], [outgoing.at[h, j] for j in FAR_OUT], relay.at[h],
            [rows_of(table, h, j) for j in NEAR_OUT], [rows_of(table, h, j) for j in FAR_OUT], halo_sems.at[h]))
        back.append(Exchange(
            device, [rows_of(acc, h, j) for j in NEAR_BACK], [rows_of(acc, h, j) for j in FAR_BACK], relay_back.at[h],
            [incoming.at[h, j] for j in NEAR_BACK], [incoming.at[h, j] for j in FAR_BACK], back_sems.at[h]))
    greeted = N_LEAF + N_BLK - 2
    for u, step in enumerate(STEPS):
        peer = lax.rem(device + step + TOTAL, TOTAL)
        there = (lax.div(peer, N_LEAF), lax.rem(peer, N_LEAF))
        greeted = greeted + halo[0].from_one[u].astype(jnp.int32)

        @pl.when(halo[0].one[u])
        def _():
            pl.semaphore_signal(barrier, inc=1, device_id=there, device_id_type=MESH)

    first = AxisSum(leaf, blk, *sums[0:8])
    cross = AxisSum(leaf, blk, *sums[8:16])
    last = Sum(leaf, blk, *sums[16:22])

    chosen = send[...]
    columns = columns_of(chosen, 4)
    nodes = lax.broadcasted_iota(jnp.int32, (128, 256), 1).astype(F32)
    choosers = [(columns[:, j : j + 1] == nodes).astype(BF16) for j in range(4)]

    def prepare(h):
        wide = jnp.concatenate([modes[c, :, 128 * h : 128 * (h + 1)] for c in range(3)], axis=1)
        parts = split3(wide)
        for j in FAR_OUT + NEAR_OUT:
            outgoing[h, j] = sum(dot(choosers[j], part, 1, 0) for part in parts)
        table[h, 0:256, :] = wide
        ext_hi[h, 0:256, :], ext_lo[h, 0:256, :] = parts[0], parts[1]

    prepare(0)
    pl.semaphore_wait(barrier, greeted)
    halo[0].send_far()
    halo[0].send_near()
    prepare(1)
    gram = sum(dot(modes[c], modes[c], 0, 0, HIGH) for c in range(3))
    first.begin(gram[0:128, 0:128], gram[128:256, 0:128], gram[128:256, 128:256])

    conn = connect[...]
    columns = columns_of(conn, 10)

    def table_id(at):
        return jnp.where(at < 256, at, jnp.where(at < 512, at + 128, jnp.where(at < 640, at - 256, at)))

    lanes = table_id(lax.broadcasted_iota(jnp.int32, (128, 768), 1)).astype(F32)
    rows = table_id(lax.broadcasted_iota(jnp.int32, (768, 128), 0))
    for k in range(10):
        pick[128 * k : 128 * (k + 1), :] = (columns[:, k : k + 1] == lanes).astype(BF16)
        place[:, 128 * k : 128 * (k + 1)] = (rows == conn[k : k + 1, :]).astype(BF16)

    halo[0].forward()
    halo[1].send_far()
    halo[1].send_near()

    def gather(h, part):
        span = slice(256 * part, 256 * (part + 1))
        if part:
            ext_hi[h, span, :], ext_lo[h, span, :] = split2(table[h, span, :])

        def body(step, carry):
            at = pl.ds(pl.multiple_of(step * 320, 320), 320)
            picked = pick[at, span]
            found = dot(picked, ext_hi[h, span, :], 1, 0) + dot(picked, ext_lo[h, span, :], 1, 0)
            taken[h, at, :] = found if part == 0 else taken[h, at, :] + found
            return carry

        lax.fori_loop(0, 4, body, 0)

    gather(0, 0)
    gather(1, 0)
    first.second()

    live = lax.broadcasted_iota(jnp.int32, (30, 128), 1) < count[0]
    source = lax.broadcasted_iota(jnp.int32, (30, 256), 0)
    target = lax.broadcasted_iota(jnp.int32, (30, 256), 1)
    wanted = lax.rem(source, 3) * 10 + lax.div(source, 3)
    spread = (lax.shift_right_logical(target, 3) == wanted).astype(BF16)
    for k in range(10):
        for c in range(3):
            block = jnp.concatenate([stiffness[k, c, l] for l in range(10)], axis=0)
            hi, lo = split2(jnp.where(live, block, 0.0))
            blocks[10 * c + k] = dot(hi, spread, 0, 0) + dot(lo, spread, 0, 0)

    keep = lax.broadcasted_iota(jnp.int32, (8, 256), 0) == lax.rem(lax.broadcasted_iota(jnp.int32, (8, 256), 1), 8)

    def assemble(g, carry):
        at = pl.ds(pl.multiple_of(g * 8, 8), 8)
        matrix = jnp.concatenate([jnp.where(keep, blocks[n, at, :], 0.0) for n in range(30)], axis=0)
        matrix_hi[g], matrix_lo[g] = split2(matrix)
        return carry

    lax.fori_loop(0, 16, assemble, 0)
    first.third()

    def multiply(h):
        def group(g, carry):
            spans = [pl.ds(pl.multiple_of(128 * k + g * 8, 8), 8) for k in range(10)]
            vectors = jnp.concatenate(
                [taken[h, spans[l], 128 * d : 128 * (d + 1)] for d in range(3) for l in range(10)]
                + [jnp.zeros((16, 128), F32)],
                axis=0,
            )
            v_hi, v_lo = split2(vectors)
            m_hi, m_lo = matrix_hi[g], matrix_lo[g]
            result = dot(m_hi, v_hi, 1, 0) + (dot(m_hi, v_lo, 1, 0) + dot(m_lo, v_hi, 1, 0))
            for c in range(3):
                for k in range(10):
                    n = 10 * c + k
                    product[spans[k], 128 * c : 128 * (c + 1)] = result[8 * n : 8 * n + 8, :]
            return carry

        lax.fori_loop(0, 16, group, 0, unroll=2)
        return split2(product[...])

    def scatter(h, halves, span):
        where = place[span, :]
        acc[h, span, :] = dot(where, halves[0], 1, 0) + dot(where, halves[1], 1, 0)

    OWN, NEAR, FAR = slice(0, 256), slice(256, 512), slice(512, 768)

    halo[0].receive_near()
    gather(0, 1)
    halo[0].receive_far()
    gather(0, 2)
    first.fourth()
    halves = multiply(0)
    scatter(0, halves, FAR)
    back[0].send_far()
    halo[1].forward()
    scatter(0, halves, NEAR)
    back[0].send_near()
    scatter(0, halves, OWN)
    first.fifth()
    halo[1].receive_near()
    gather(1, 1)
    halo[1].receive_far()
    gather(1, 2)
    halves = multiply(1)
    scatter(1, halves, FAR)
    back[1].send_far()
    back[0].forward()
    scatter(1, halves, NEAR)
    back[1].send_near()
    scatter(1, halves, OWN)

    def against(a, b):
        spans = [slice(128 * c, 128 * (c + 1)) for c in range(3)]
        return sum(dot(acc[a, :, s], table[b, :, s], 0, 0, HIGH) for s in spans)

    cross.begin(against(0, 0), against(1, 0), against(1, 1))

    first.end()
    factor_start(work, unpack(first.total[...]))
    factor(work, 0, 64)
    cross.second()
    factor(work, 64, 128)
    back[1].forward()
    factor(work, 128, 192)
    cross.third()
    factor(work, 192, 256)
    r_out[...] = upper(work[:, 0:SIDE])
    inv = work[:, SIDE:]
    cross.fourth()
    for c in range(3):
        q_out[c] = dot(modes[c], inv, 1, 1, HIGH)

    rows = lax.broadcasted_iota(jnp.int32, (256, 128), 0)
    to_own = jnp.concatenate([(rows == chosen[j : j + 1, :]).astype(BF16) for j in range(4)], axis=1)

    def complete(h):
        back[h].receive_near()
        back[h].receive_far()
        parts = split3(jnp.concatenate([incoming[h, j] for j in range(4)], axis=0))
        whole = acc[h, OWN, :] + sum(dot(to_own, part, 1, 0) for part in parts)
        for c in range(3):
            stiff[c, :, 128 * h : 128 * (h + 1)] = whole[:, 128 * c : 128 * (c + 1)]

    complete(0)
    top = sum(dot(stiff[c, :, 0:128], stiff[c, :, 0:128], 0, 0, HIGH) for c in range(3))
    cross.fifth()
    complete(1)
    bottom = sum(dot(stiff[c, :, 128:256], stiff[c], 0, 0, HIGH) for c in range(3))
    last.begin(top, bottom[:, 0:128], bottom[:, 128:256])

    cross.end()
    low = dot(unpack(cross.total[...]), inv, 1, 1, HIGH)
    low_out[...] = low
    last.across()
    for c in range(3):
        rest_out[c] = stiff[c] - dot(q_out[c], low, 1, 1, HIGH)
    last.gather()
    for h in range(2):
        halo[h].drain()
        back[h].drain()
    first.drain()
    cross.drain()
    last.end()
    last.drain()
    g22_out[...] = last.total[...]


def up_to_last_gram(count, modes, stiffness, connect, send):
    square = jax.ShapeDtypeStruct((SIDE, SIDE), F32)
    tall = jax.ShapeDtypeStruct((3, 256, 256), F32)
    rows = pltpu.VMEM((2, 4, 128, 384), F32)
    table = pltpu.VMEM((2, 768, 384), F32)
    relay = pltpu.VMEM((2, 2, 128, 384), F32)
    sems = pltpu.SemaphoreType.DMA((2, 2, 3, 2))
    return pl.pallas_call(
        main_kernel,
        out_shape=[jax.ShapeDtypeStruct((384, 128), F32), square, tall, square, tall],
        in_specs=[SMEM] + [VMEM] * 4,
        out_specs=[VMEM] * 5,
        scratch_shapes=[
            rows, table, relay, table, rows, relay, sems, sems,
            pltpu.VMEM((2, 768, 384), BF16),
            pltpu.VMEM((2, 768, 384), BF16),
            pltpu.VMEM((1280, 768), BF16),
            pltpu.VMEM((768, 1280), BF16),
            pltpu.VMEM((2, 1280, 384), F32),
            pltpu.VMEM((30, 128, 256), F32),
            pltpu.VMEM((16, 240, 256), BF16),
            pltpu.VMEM((16, 240, 256), BF16),
            pltpu.VMEM((1280, 384), F32),
            pltpu.VMEM((3, 256, 256), F32),
            pltpu.VMEM((SIDE, 2 * SIDE), F32),
        ] + axis_sum_scratch() * 2 + sum_scratch(),
        compiler_params=pltpu.CompilerParams(collective_id=1, has_side_effects=True, vmem_limit_bytes=LIMIT),
        name="up_to_last_gram",
    )(count, modes, stiffness, connect, send)


def second_kernel(scale, g22, low, r11, q1, rest, q_out, r_out, work):
    lower = low[...]
    factor_start(work, unpack(g22[...]) - dot(lower, lower, 1, 1, HIGH))
    factor(work, 0, SIDE)
    r_out[0:SIDE, 0:SIDE] = r11[...] / scale
    r_out[0:SIDE, SIDE:] = lower.T / scale
    r_out[SIDE:, 0:SIDE] = jnp.zeros((SIDE, SIDE), F32)
    r_out[SIDE:, SIDE:] = upper(work[:, 0:SIDE]) / scale
    inv = work[:, SIDE:]
    for c in range(3):
        q_out[c, :, 0:SIDE] = q1[c] * scale
        q_out[c, :, SIDE:] = dot(rest[c], inv, 1, 1, HIGH) * scale


def second(scale, *operands):
    return pl.pallas_call(
        functools.partial(second_kernel, scale),
        out_shape=[jax.ShapeDtypeStruct((3, 256, 512), F32), jax.ShapeDtypeStruct((512, 512), F32)],
        in_specs=[VMEM] * len(operands),
        out_specs=[VMEM] * 2,
        scratch_shapes=[pltpu.VMEM((SIDE, 2 * SIDE), F32)],
        compiler_params=pltpu.CompilerParams(vmem_limit_bytes=LIMIT),
        name="second_factor",
    )(*operands)


def shards(modes, stiffness, connect, send_list, elem_count):
    modes = jnp.transpose(modes, (1, 0, 2))
    g22, low, rest, r11, q1 = up_to_last_gram(elem_count, modes, stiffness, connect, send_list[0])
    scale = float((3 * 256 * lax.axis_size("blk") * lax.axis_size("leaf")) ** 0.5)
    q, r = second(scale, g22, low, r11, q1, rest)
    return (jnp.transpose(q, (1, 0, 2)), r)


def solution(mesh):
    placed = (
        P(("blk", "leaf"), None, None),
        P(None, None, None, None, ("blk", "leaf")),
        P(None, ("blk", "leaf")),
        P(("blk", "leaf"), None, None),
        P(("blk", "leaf")),
    )
    return jax.shard_map(
        shards,
        mesh=mesh,
        in_specs=placed,
        out_specs=(P(("blk", "leaf"), None, None), P()),
        check_vma=False,
    )
```

time: 613 us -> 126 us (0.21); the launches traced: 602 us -> 126 us
  other arithmetic: 280 us -> 0 us
  waiting for transfers between devices: 170 us -> 0 us
  Pallas kernels: 0 us -> 124 us
  local copies, waits for them, and re-layouts: 73.8 us -> 0 us
  matrix products: 32.7 us -> 0 us
  starting transfers between devices: 26.4 us -> 0 us
  between operations: 18.2 us -> 1.29 us
    psum x1 -> x0, waiting for transfers between devices: 166 us -> none  [shards(): total_gram = lax.psum(local_gram, ('blk', 'leaf'))]
    scatter-add x5 -> x0, other arithmetic: 157 us -> none  [the longest x1 94.6 us: element_block(): return accumulated.at[connect].add(product)]
    pallas_call x0 -> x2, Pallas kernels: none -> 124 us  [the longest x1 111 us: up_to_last_gram(): pl.pallas_call(main_kernel, out_shape=[jax.ShapeDtypeStruct((384, 128), F...]
    another operation x16 -> x0, other arithmetic: 118 us -> none  [the longest x14 78.6 us: shards(): lower = jnp.linalg.cholesky(total_gram)]
    ppermute x8 -> x0, starting transfers between devices: 26.4 us -> none  [from_behind(): lax.ppermute(value, axis, [(source, source + steps) for source in range(i...]
    dot_general x2 -> x0, matrix products: 18.1 us -> none  [the longest x1 14.4 us: element_block(): jnp.einsum('kcldE,lEdm->kEcm', blocks, gathered, precision=lax.Precision....]
    another operation x13 -> x0, matrix products: 14.6 us -> none  [the longest x7 9.1 us: shards(): solved = jax.scipy.linalg.solve_triangular(lower, flat.T, lower=True).T]
    gather x5 -> x0, local copies, waits for them, and re-layouts: 14.4 us -> none  [the longest x4 8.29 us: shards(): outgoing = modes[send_table[j]]]
  transfers between devices with their start and end apart: 9 -> 0, of which waited for: 3 -> 0; matrix products, arithmetic and copies ran while one was open for 12% -> 0% of each run, Pallas kernels for 0% -> 0%
where the time goes in v1:
time: 126 us
  Pallas kernels  124 us (98%)
  between operations  1.29 us (1%)
    pallas_call x1, Pallas kernels, up_to_last_gram(): pl.pallas_call(main_kernel, out_shape=[jax.ShapeDtypeStruct((384, 128), F...  111 us
    pallas_call x1, Pallas kernels, second(): pl.pallas_call(functools.partial(second_kernel, scale), out_shape=[jax.Sh...  13.2 us

profile of v1, /device:TPU:0, one launch (start us, length us, event | category | flops | bytes accessed | tf_op | source)
XLA Modules:
  0.0 125.6 jit_solution(9469641646202322430)
XLA Ops:
  1.3 111.1 %up_to_last_gram.1 = (f32[384,128]{1,0:T(8,128)}, f32[256,256]{1,0:T(8,128)}, f32[3,256,256]{2,1,0:T(8,128)}, f32[256,256]{1,0:T(8,128)}, f32[3,256,256]{2,1,0:T(8,128)}) custom-call(s32[1]{0:T(128)S(6)} %copy.7.count, f32[3,256,256]{2,1,0:T(8,128)} %bitcast.3, f32[10,3,10,3,128]{4,3,2,1,0:T(4,128)} %stiffness.1, s32[10,128]{1,0:T(8,128)} %connect.1, ...), custom_call_target="tpu_custom_call" | custom-call | tf_op jit(solution)/shard_map/up_to_last_gram/pallas_call | solution.py:564
  112.4 13.2 %second_factor.1 = (f32[3,256,512]{2,1,0:T(8,128)}, f32[512,512]{1,0:T(8,128)}) custom-call(f32[384,128]{1,0:T(8,128)} %get-tuple-element.9.g22, f32[256,256]{1,0:T(8,128)} %get-tuple-element.10.low, f32[256,256]{1,0:T(8,128)} %get-tuple-element.11.r11, f32[3,256,256]{2,1,0:T(8,128)} %get-tuple-element.12.q1, f32[3,256,256]{2,1,0:T(8,128)} %get-tuple-element.13.rest), custom_call_target="tpu_custom_call" | custom-call | tf_op jit(solution)/shard_map/second_factor/pallas_call | solution.py:603

commit v2 on v1

--- a/solution.py
+++ b/solution.py
@@ -39,7 +39,6 @@
 
 N_LEAF = 16
 N_BLK = 8
-CHUNK = 24
 
 
 def greet(leaf, blk):
@@ -53,15 +52,16 @@
 
 class Sum:
     def __init__(self, leaf, blk, local, near, far, total, leaf_sems, blk_sems):
-        self.leaf, self.blk = leaf, blk
+        size = local.shape[0] // N_LEAF
+        self.blk = blk
         self.local, self.near, self.far, self.total = local, near, far, total
-        mine = pl.ds(pl.multiple_of(leaf * CHUNK, 8), CHUNK)
+        mine = pl.ds(pl.multiple_of(leaf * size, 8), size)
         self.mine = mine
         self.spread, self.cross, self.collect = [], [], []
         for k in range(1, N_LEAF):
             peer = lax.rem(leaf + k, N_LEAF)
             self.spread.append(pltpu.make_async_remote_copy(
-                src_ref=local.at[pl.ds(pl.multiple_of(peer * CHUNK, 8), CHUNK)], dst_ref=near.at[k],
+                src_ref=local.at[pl.ds(pl.multiple_of(peer * size, 8), size)], dst_ref=near.at[k],
                 send_sem=leaf_sems.at[0, k], recv_sem=leaf_sems.at[1, k], device_id={"leaf": peer}, device_id_type=MESH))
             self.collect.append(pltpu.make_async_remote_copy(
                 src_ref=total.at[mine], dst_ref=total.at[mine],
@@ -72,10 +72,9 @@
                 src_ref=far.at[blk], dst_ref=far.at[blk],
                 send_sem=blk_sems.at[0, k], recv_sem=blk_sems.at[1, k], device_id={"blk": peer}, device_id_type=MESH))
 
-    def begin(self, top, low, bottom):
-        self.local[0:128, :] = top
-        self.local[128:256, :] = low
-        self.local[256:384, :] = bottom
+    def begin(self, *parts):
+        for n, part in enumerate(parts):
+            self.local[128 * n : 128 * (n + 1), :] = part
         for copy in self.spread:
             copy.start()
 
@@ -107,114 +106,20 @@
             copy.wait_send()
 
 
-def sum_scratch():
+def sum_scratch(parts):
+    size = 128 * parts // N_LEAF
     return [
-        pltpu.VMEM((384, 128), F32),
-        pltpu.VMEM((N_LEAF, CHUNK, 128), F32),
-        pltpu.VMEM((N_BLK, CHUNK, 128), F32),
-        pltpu.VMEM((384, 128), F32),
+        pltpu.VMEM((128 * parts, 128), F32),
+        pltpu.VMEM((N_LEAF, size, 128), F32),
+        pltpu.VMEM((N_BLK, size, 128), F32),
+        pltpu.VMEM((128 * parts, 128), F32),
         pltpu.SemaphoreType.DMA((4, N_LEAF)),
         pltpu.SemaphoreType.DMA((2, N_BLK)),
     ]
 
 
-class AxisSum:
-    def __init__(self, leaf, blk, local, along_x, part, along_y, far, total, sems, blk_sems):
-        self.blk, self.local, self.part, self.total = blk, local, part, total
-        self.along_x, self.along_y, self.far = along_x, along_y, far
-        x, y = lax.div(leaf, 4), lax.rem(leaf, 4)
-        wide, slim = 4 * CHUNK, CHUNK
-        self.wide = pl.ds(pl.multiple_of(x * wide, 8), wide)
-        self.slim = pl.ds(pl.multiple_of(y * slim, 8), slim)
-        self.mine = pl.ds(pl.multiple_of(leaf * slim, 8), slim)
-        self.stages = [[], [], [], [], []]
-
-        def copy(stage, k, src, dst, sem, peer):
-            self.stages[stage].append(pltpu.make_async_remote_copy(
-                src_ref=src, dst_ref=dst, send_sem=sem.at[0, k], recv_sem=sem.at[1, k],
-                device_id=peer, device_id_type=MESH))
-
-        for k in range(1, 4):
-            px, py = lax.rem(x + k, 4), lax.rem(y + k, 4)
-            beside, above = {"leaf": px * 4 + y}, {"leaf": x * 4 + py}
-            copy(0, k, local.at[pl.ds(pl.multiple_of(px * wide, 8), wide)], along_x.at[k], sems.at[0], beside)
-            copy(1, k, part.at[pl.ds(pl.multiple_of(py * slim, 8), slim)], along_y.at[k], sems.at[1], above)
-            copy(3, k, total.at[self.mine], total.at[self.mine], sems.at[2], above)
-            copy(4, k, total.at[self.wide], total.at[self.wide], sems.at[3], beside)
-        for k in range(1, N_BLK):
-            copy(2, k, far.at[blk], far.at[blk], blk_sems, {"blk": lax.rem(blk + k, N_BLK)})
-
-    def start(self, stage):
-        for copy in self.stages[stage]:
-            copy.start()
-
-    def wait(self, stage):
-        for copy in self.stages[stage]:
-            copy.wait_recv()
-
-    def begin(self, top, low, bottom):
-        self.local[0:128, :] = top
-        self.local[128:256, :] = low
-        self.local[256:384, :] = bottom
-        self.start(0)
-
-    def second(self):
-        self.wait(0)
-        part = self.local[self.wide, :]
-        for k in range(1, 4):
-            part = part + self.along_x[k]
-        self.part[...] = part
-        self.start(1)
-
-    def third(self):
-        self.wait(1)
-        part = self.part[self.slim, :]
-        for k in range(1, 4):
-            part = part + self.along_y[k]
-        self.far[self.blk] = part
-        self.start(2)
-
-    def fourth(self):
-        self.wait(2)
-        part = self.far[0]
-        for b in range(1, N_BLK):
-            part = part + self.far[b]
-        self.total[self.mine, :] = part
-        self.start(3)
-
-    def fifth(self):
-        self.wait(3)
-        self.start(4)
-
-    def end(self):
-        self.wait(4)
-
-    def drain(self):
-        for stage in self.stages:
-            for copy in stage:
-                copy.wait_send()
-
-
-def axis_sum_scratch():
-    return [
-        pltpu.VMEM((384, 128), F32),
-        pltpu.VMEM((4, 4 * CHUNK, 128), F32),
-        pltpu.VMEM((4 * CHUNK, 128), F32),
-        pltpu.VMEM((4, CHUNK, 128), F32),
-        pltpu.VMEM((N_BLK, CHUNK, 128), F32),
-        pltpu.VMEM((384, 128), F32),
-        pltpu.SemaphoreType.DMA((4, 2, 4)),
-        pltpu.SemaphoreType.DMA((2, N_BLK)),
-    ]
-
-
-SIDE = 256
+SIDE = 128
 BLOCK = 64
-
-
-def unpack(packed):
-    top, low, bottom = packed[0:128, :], packed[128:256, :], packed[256:384, :]
-    return jnp.concatenate([jnp.concatenate([top, low.T], axis=1), jnp.concatenate([low, bottom], axis=1)], axis=0)
 
 
 def factor_start(work, gram):
@@ -224,46 +129,44 @@
     ).astype(F32)
 
 
-def factor(work, first, last):
+def factor(work, start):
     sub = lax.broadcasted_iota(jnp.int32, (8, 128), 0)
-    for start in range(first, last, BLOCK):
-        left = start // 128 * 128
-        right = SIDE + -(-(start + BLOCK) // 128) * 128
-        if start:
-            update = dot(work[0:start, start : start + BLOCK], work[0:start, left:right], 0, 0, HIGH)
-            work[start : start + BLOCK, left:right] = work[start : start + BLOCK, left:right] - update
-        tiles = (right - left) // 128
-        count = BLOCK // 8
-        x = [[work[start + 8 * t : start + 8 * t + 8, left + 128 * i : left + 128 * (i + 1)] for i in range(tiles)]
-             for t in range(count)]
-        for p in range(count):
-            tile, lane = divmod(start + 8 * p - left, 128)
-            rest = range(p, count)
-            col = [{t: jnp.broadcast_to(x[t][tile][:, lane + j : lane + j + 1], (8, 128)) for t in rest} for j in range(8)]
-            entry = {(i, k): jnp.broadcast_to(col[k][p][i : i + 1, :], (8, 128)) for k in range(8) for i in range(k, 8)}
-            for j in range(8):
-                inverse = lax.rsqrt(entry[j, j])
-                scaled = {k: entry[k, j] * inverse for k in range(j + 1, 8)}
-                low = {t: col[j][t] * inverse for t in rest}
-                for k in range(j + 1, 8):
-                    for i in range(k, 8):
-                        entry[i, k] = entry[i, k] - scaled[i] * scaled[k]
-                    for t in rest:
-                        col[k][t] = col[k][t] - low[t] * scaled[k]
-                for i in range(tiles):
-                    row = jnp.broadcast_to(x[p][i][j : j + 1, :], (8, 128)) * inverse
-                    for t in rest:
-                        moved = x[t][i] - low[t] * row
-                        if t == p:
-                            moved = jnp.where(sub > j, moved, jnp.where(sub == j, row, x[t][i]))
-                        x[t][i] = moved
+    if start:
+        update = dot(work[0:start, start : start + BLOCK], work[0:start, :], 0, 0, HIGH)
+        work[start : start + BLOCK, :] = work[start : start + BLOCK, :] - update
+    count = BLOCK // 8
+    tiles = 2
+    x = [[work[start + 8 * t : start + 8 * t + 8, 128 * i : 128 * (i + 1)] for i in range(tiles)] for t in range(count)]
+    for p in range(count):
+        lane = start + 8 * p
+        rest = range(p, count)
+        col = [{t: jnp.broadcast_to(x[t][0][:, lane + j : lane + j + 1], (8, 128)) for t in rest} for j in range(8)]
+        for j in range(8):
+            inverse = lax.rsqrt(jnp.broadcast_to(col[j][p][j : j + 1, :], (8, 128)))
+            low = {t: col[j][t] * inverse for t in rest}
+            for k in range(j + 1, 8):
+                pivot = jnp.broadcast_to(low[p][k : k + 1, :], (8, 128))
+                for t in rest:
+                    col[k][t] = col[k][t] - low[t] * pivot
             for i in range(tiles):
-                work[start + 8 * p : start + 8 * p + 8, left + 128 * i : left + 128 * (i + 1)] = x[p][i]
-
-
-def upper(x):
+                row = jnp.broadcast_to(x[p][i][j : j + 1, :], (8, 128)) * inverse
+                for t in rest:
+                    moved = x[t][i] - low[t] * row
+                    if t == p:
+                        moved = jnp.where(sub > j, moved, jnp.where(sub == j, row, x[t][i]))
+                    x[t][i] = moved
+        for i in range(tiles):
+            work[start + 8 * p : start + 8 * p + 8, 128 * i : 128 * (i + 1)] = x[p][i]
+
+
+def factored(work):
     keep = lax.broadcasted_iota(jnp.int32, (SIDE, SIDE), 0) <= lax.broadcasted_iota(jnp.int32, (SIDE, SIDE), 1)
-    return jnp.where(keep, x, 0.0)
+    return jnp.where(keep, work[:, 0:SIDE], 0.0), work[:, SIDE:]
+
+
+def dot3(a, b, ca, cb):
+    (ah, al), (bh, bl) = split2(a), split2(b)
+    return dot(ah, bh, ca, cb) + (dot(ah, bl, ca, cb) + dot(al, bh, ca, cb))
 
 
 TOTAL = N_LEAF * N_BLK
@@ -338,7 +241,7 @@
 NEAR_BACK, FAR_BACK = (2, 1), (3, 0)
 
 
-def main_kernel(count, modes, stiffness, connect, send, g22_out, low_out, rest_out, r_out, q_out,
+def main_kernel(scale, count, modes, stiffness, connect, send, bottom_out, low_out, rest_out, r_out, top_out, inv_out, q_out,
                 outgoing, table, relay, acc, incoming, relay_back, halo_sems, back_sems,
                 ext_hi, ext_lo, pick, place, taken, blocks, matrix_hi, matrix_lo, product, stiff, work, *sums):
     leaf, blk = lax.axis_index("leaf"), lax.axis_index("blk")
@@ -366,9 +269,7 @@
         def _():
             pl.semaphore_signal(barrier, inc=1, device_id=there, device_id_type=MESH)
 
-    first = AxisSum(leaf, blk, *sums[0:8])
-    cross = AxisSum(leaf, blk, *sums[8:16])
-    last = Sum(leaf, blk, *sums[16:22])
+    first, cross, top, bottom = (Sum(leaf, blk, *sums[6 * i : 6 * i + 6]) for i in range(4))
 
     chosen = send[...]
     columns = columns_of(chosen, 4)
@@ -388,7 +289,7 @@
     halo[0].send_far()
     halo[0].send_near()
     prepare(1)
-    gram = sum(dot(modes[c], modes[c], 0, 0, HIGH) for c in range(3))
+    gram = sum(dot3(modes[c].T, modes[c], 1, 0) for c in range(3))
     first.begin(gram[0:128, 0:128], gram[128:256, 0:128], gram[128:256, 128:256])
 
     conn = connect[...]
@@ -423,7 +324,6 @@
 
     gather(0, 0)
     gather(1, 0)
-    first.second()
 
     live = lax.broadcasted_iota(jnp.int32, (30, 128), 1) < count[0]
     source = lax.broadcasted_iota(jnp.int32, (30, 256), 0)
@@ -445,7 +345,6 @@
         return carry
 
     lax.fori_loop(0, 16, assemble, 0)
-    first.third()
 
     def multiply(h):
         def group(g, carry):
@@ -477,19 +376,19 @@
     gather(0, 1)
     halo[0].receive_far()
     gather(0, 2)
-    first.fourth()
     halves = multiply(0)
+    first.across()
     scatter(0, halves, FAR)
     back[0].send_far()
     halo[1].forward()
     scatter(0, halves, NEAR)
     back[0].send_near()
     scatter(0, halves, OWN)
-    first.fifth()
     halo[1].receive_near()
     gather(1, 1)
     halo[1].receive_far()
     gather(1, 2)
+    first.gather()
     halves = multiply(1)
     scatter(1, halves, FAR)
     back[1].send_far()
@@ -498,26 +397,20 @@
     back[1].send_near()
     scatter(1, halves, OWN)
 
-    def against(a, b):
-        spans = [slice(128 * c, 128 * (c + 1)) for c in range(3)]
-        return sum(dot(acc[a, :, s], table[b, :, s], 0, 0, HIGH) for s in spans)
-
-    cross.begin(against(0, 0), against(1, 0), against(1, 1))
-
-    first.end()
-    factor_start(work, unpack(first.total[...]))
-    factor(work, 0, 64)
-    cross.second()
-    factor(work, 64, 128)
-    back[1].forward()
-    factor(work, 128, 192)
-    cross.third()
-    factor(work, 192, 256)
-    r_out[...] = upper(work[:, 0:SIDE])
-    inv = work[:, SIDE:]
-    cross.fourth()
+    lower, diagonal = [], 0.0
     for c in range(3):
-        q_out[c] = dot(modes[c], inv, 1, 1, HIGH)
+        at = slice(128 * c, 128 * (c + 1))
+        tables = [jnp.concatenate([ext[0, :, at], ext[1, :, at]], axis=1) for ext in (ext_hi, ext_lo)]
+        for h in range(2):
+            hi, lo = split2(acc[h, :, at].T)
+            t_hi, t_lo = (t if h else t[:, 0:128] for t in tables)
+            found = dot(hi, t_hi, 1, 0) + (dot(hi, t_lo, 1, 0) + dot(lo, t_hi, 1, 0))
+            if h:
+                lower.append(found)
+            else:
+                diagonal = diagonal + found
+    lower = sum(lower)
+    cross.begin(diagonal, lower[:, 0:128], lower[:, 128:256])
 
     rows = lax.broadcasted_iota(jnp.int32, (256, 128), 0)
     to_own = jnp.concatenate([(rows == chosen[j : j + 1, :]).astype(BF16) for j in range(4)], axis=1)
@@ -525,47 +418,81 @@
     def complete(h):
         back[h].receive_near()
         back[h].receive_far()
-        parts = split3(jnp.concatenate([incoming[h, j] for j in range(4)], axis=0))
+        parts = split2(jnp.concatenate([incoming[h, j] for j in range(4)], axis=0))
         whole = acc[h, OWN, :] + sum(dot(to_own, part, 1, 0) for part in parts)
         for c in range(3):
             stiff[c, :, 128 * h : 128 * (h + 1)] = whole[:, 128 * c : 128 * (c + 1)]
 
+    first.end()
+    factor_start(work, first.total[0:128, :])
+    factor(work, 0)
+    back[1].forward()
+    factor(work, 64)
+    r00, i00 = factored(work)
     complete(0)
-    top = sum(dot(stiff[c, :, 0:128], stiff[c, :, 0:128], 0, 0, HIGH) for c in range(3))
-    cross.fifth()
+    top.begin(sum(dot3(stiff[c, :, 0:128].T, stiff[c, :, 0:128], 1, 0) for c in range(3)))
+    r01 = dot(i00, first.total[128:256, :], 1, 1, HIGH)
+    factor_start(work, first.total[256:384, :] - dot(r01, r01, 0, 0, HIGH))
+    factor(work, 0)
+    factor(work, 64)
+    r11, i11 = factored(work)
+    r_out[0:128, 0:128], r_out[0:128, 128:256] = r00, r01
+    r_out[128:256, 0:128], r_out[128:256, 128:256] = jnp.zeros((SIDE, SIDE), F32), r11
+    i10 = dot(i11, dot(r01, i00, 0, 0, HIGH), 1, 0, HIGH)
+    inv = jnp.concatenate(
+        [jnp.concatenate([i00, jnp.zeros((SIDE, SIDE), F32)], axis=1), jnp.concatenate([-i10, i11], axis=1)], axis=0)
+    cross.across()
+    for c in range(3):
+        q_out[c, :, 0:256] = dot3(modes[c], inv, 1, 1) * scale
+
     complete(1)
-    bottom = sum(dot(stiff[c, :, 128:256], stiff[c], 0, 0, HIGH) for c in range(3))
-    last.begin(top, bottom[:, 0:128], bottom[:, 128:256])
-
+    both = sum(dot3(stiff[c, :, 128:256].T, stiff[c], 1, 0) for c in range(3))
+    bottom.begin(both[:, 0:128], both[:, 128:256])
+    cross.gather()
+    top.across()
+    top.gather()
     cross.end()
-    low = dot(unpack(cross.total[...]), inv, 1, 1, HIGH)
+    crossed = cross.total
+    gram = jnp.concatenate(
+        [jnp.concatenate([crossed[0:128, :], crossed[128:256, :].T], axis=1),
+         jnp.concatenate([crossed[128:256, :], crossed[256:384, :]], axis=1)], axis=0)
+    low = dot(gram, inv, 1, 1, HIGH)
     low_out[...] = low
-    last.across()
+    top.end()
+    factor_start(work, top.total[...] - dot(low[0:128, :], low[0:128, :], 1, 1, HIGH))
+    factor(work, 0)
+    bottom.across()
+    factor(work, 64)
+    bottom.gather()
+    r22, i22 = factored(work)
+    top_out[...] = r22
+    inv_out[...] = i22
     for c in range(3):
-        rest_out[c] = stiff[c] - dot(q_out[c], low, 1, 1, HIGH)
-    last.gather()
+        rest = stiff[c] - dot3(q_out[c, :, 0:256], low / scale, 1, 1)
+        q_out[c, :, 256:384] = dot3(rest[:, 0:128], i22, 1, 1) * scale
+        rest_out[c] = rest[:, 128:256]
     for h in range(2):
         halo[h].drain()
         back[h].drain()
     first.drain()
     cross.drain()
-    last.end()
-    last.drain()
-    g22_out[...] = last.total[...]
-
-
-def up_to_last_gram(count, modes, stiffness, connect, send):
-    square = jax.ShapeDtypeStruct((SIDE, SIDE), F32)
-    tall = jax.ShapeDtypeStruct((3, 256, 256), F32)
+    top.drain()
+    bottom.end()
+    bottom.drain()
+    bottom_out[...] = bottom.total[...]
+
+
+def up_to_last_gram(scale, count, modes, stiffness, connect, send):
+    shapes = ((256, 128), (256, 256), (3, 256, 128), (256, 256), (128, 128), (128, 128), (3, 256, 384))
     rows = pltpu.VMEM((2, 4, 128, 384), F32)
     table = pltpu.VMEM((2, 768, 384), F32)
     relay = pltpu.VMEM((2, 2, 128, 384), F32)
     sems = pltpu.SemaphoreType.DMA((2, 2, 3, 2))
     return pl.pallas_call(
-        main_kernel,
-        out_shape=[jax.ShapeDtypeStruct((384, 128), F32), square, tall, square, tall],
+        functools.partial(main_kernel, scale),
+        out_shape=[jax.ShapeDtypeStruct(shape, F32) for shape in shapes],
         in_specs=[SMEM] + [VMEM] * 4,
-        out_specs=[VMEM] * 5,
+        out_specs=[VMEM] * len(shapes),
         scratch_shapes=[
             rows, table, relay, table, rows, relay, sems, sems,
             pltpu.VMEM((2, 768, 384), BF16),
@@ -579,33 +506,54 @@
             pltpu.VMEM((1280, 384), F32),
             pltpu.VMEM((3, 256, 256), F32),
             pltpu.VMEM((SIDE, 2 * SIDE), F32),
-        ] + axis_sum_scratch() * 2 + sum_scratch(),
+        ] + sum_scratch(3) + sum_scratch(3) + sum_scratch(1) + sum_scratch(2),
         compiler_params=pltpu.CompilerParams(collective_id=1, has_side_effects=True, vmem_limit_bytes=LIMIT),
         name="up_to_last_gram",
     )(count, modes, stiffness, connect, send)
 
 
-def second_kernel(scale, g22, low, r11, q1, rest, q_out, r_out, work):
-    lower = low[...]
-    factor_start(work, unpack(g22[...]) - dot(lower, lower, 1, 1, HIGH))
-    factor(work, 0, SIDE)
-    r_out[0:SIDE, 0:SIDE] = r11[...] / scale
-    r_out[0:SIDE, SIDE:] = lower.T / scale
-    r_out[SIDE:, 0:SIDE] = jnp.zeros((SIDE, SIDE), F32)
-    r_out[SIDE:, SIDE:] = upper(work[:, 0:SIDE]) / scale
-    inv = work[:, SIDE:]
+def second_kernel(scale, bottom, low, r_first, r_top, i_top, rest, q_in, q_out, r_out, work, top_columns, last, sems):
+    done = pltpu.make_async_copy(q_in, q_out.at[:, :, pl.ds(0, 384)], sems.at[0])
+    fetch = pltpu.make_async_copy(q_in.at[:, :, pl.ds(256, 128)], top_columns, sems.at[1])
+    done.start()
+    fetch.start()
+    low0, low1 = low[0:128, :], low[128:256, :]
+    side = bottom[0:128, :] - dot(low1, low0, 1, 1, HIGH)
+    r01 = dot(i_top[...], side, 1, 1, HIGH)
+    factor_start(work, bottom[128:256, :] - dot(low1, low1, 1, 1, HIGH) - dot(r01, r01, 0, 0, HIGH))
+    factor(work, 0)
+    r_out[0:256, 0:256] = r_first[...] / scale
+    r_out[0:256, 256:512] = low[...].T / scale
+    r_out[256:512, 0:256] = jnp.zeros((256, 256), F32)
+    r_out[256:384, 256:384] = r_top[...] / scale
+    r_out[256:384, 384:512] = r01 / scale
+    r_out[384:512, 256:384] = jnp.zeros((128, 128), F32)
+    factor(work, 64)
+    r11, i11 = factored(work)
+    r_out[384:512, 384:512] = r11 / scale
+    fetch.wait()
     for c in range(3):
-        q_out[c, :, 0:SIDE] = q1[c] * scale
-        q_out[c, :, SIDE:] = dot(rest[c], inv, 1, 1, HIGH) * scale
+        left = rest[c] - dot3(top_columns[c], r01 / scale, 1, 0)
+        last[c] = dot3(left, i11, 1, 1) * scale
+    place = pltpu.make_async_copy(last, q_out.at[:, :, pl.ds(384, 128)], sems.at[2])
+    place.start()
+    place.wait()
+    done.wait()
 
 
 def second(scale, *operands):
+    anywhere = pl.BlockSpec(memory_space=pl.ANY)
     return pl.pallas_call(
         functools.partial(second_kernel, scale),
         out_shape=[jax.ShapeDtypeStruct((3, 256, 512), F32), jax.ShapeDtypeStruct((512, 512), F32)],
-        in_specs=[VMEM] * len(operands),
-        out_specs=[VMEM] * 2,
-        scratch_shapes=[pltpu.VMEM((SIDE, 2 * SIDE), F32)],
+        in_specs=[VMEM] * 6 + [anywhere],
+        out_specs=[anywhere, VMEM],
+        scratch_shapes=[
+            pltpu.VMEM((SIDE, 2 * SIDE), F32),
+            pltpu.VMEM((3, 256, 128), F32),
+            pltpu.VMEM((3, 256, 128), F32),
+            pltpu.SemaphoreType.DMA((3,)),
+        ],
         compiler_params=pltpu.CompilerParams(vmem_limit_bytes=LIMIT),
         name="second_factor",
     )(*operands)
@@ -613,9 +561,10 @@
 
 def shards(modes, stiffness, connect, send_list, elem_count):
     modes = jnp.transpose(modes, (1, 0, 2))
-    g22, low, rest, r11, q1 = up_to_last_gram(elem_count, modes, stiffness, connect, send_list[0])
     scale = float((3 * 256 * lax.axis_size("blk") * lax.axis_size("leaf")) ** 0.5)
-    q, r = second(scale, g22, low, r11, q1, rest)
+    bottom, low, rest, r_first, r_top, i_top, q = up_to_last_gram(
+        scale, elem_count, modes, stiffness, connect, send_list[0])
+    q, r = second(scale, bottom, low, r_first, r_top, i_top, rest, q)
     return (jnp.transpose(q, (1, 0, 2)), r)
 
 

time: 126 us -> 141 us (1.12)
  Pallas kernels: 124 us -> 139 us
    pallas_call x1, Pallas kernels: 13.2 us -> 39.1 us  [second(): pl.pallas_call(functools.partial(second_kernel, scale), out_shape=[jax.Sh...]
    pallas_call x1, Pallas kernels: 111 us -> 99.8 us  [up_to_last_gram(): pl.pallas_call(functools.partial(main_kernel, scale), out_shape=[jax.Shap...]
where the time goes in v2:
time: 141 us; the launch traced here: 140 us
  Pallas kernels  139 us (99%)
  between operations  1.47 us (1%)
    pallas_call x1, Pallas kernels, up_to_last_gram(): pl.pallas_call(functools.partial(main_kernel, scale), out_shape=[jax.Shap...  99.8 us
    pallas_call x1, Pallas kernels, second(): pl.pallas_call(functools.partial(second_kernel, scale), out_shape=[jax.Sh...  39.1 us

profile of v2, /device:TPU:0, one launch (start us, length us, event | category | flops | bytes accessed | tf_op | source)
XLA Modules:
  0.0 140.4 jit_solution(6409955203454853326)
XLA Ops:
  1.3 99.8 %up_to_last_gram.1 = (f32[256,128]{1,0:T(8,128)}, f32[256,256]{1,0:T(8,128)}, f32[3,256,128]{2,1,0:T(8,128)}, f32[256,256]{1,0:T(8,128)}, f32[128,128]{1,0:T(8,1...) custom-call(s32[1]{0:T(128)S(6)} %copy.7.count, f32[3,256,256]{2,1,0:T(8,128)} %bitcast.3, ...), custom_call_target="tpu_custom_call" | custom-call | tf_op jit(solution)/shard_map/up_to_last_gram/pallas_call | solution.py:491
  101.1 39.1 %second_factor.1 = (f32[3,256,512]{2,1,0:T(8,128)}, f32[512,512]{1,0:T(8,128)}) custom-call(f32[256,128]{1,0:T(8,128)} %get-tuple-element.11.bottom, f32[256,256]{1,0:T(8,128)} %get-tuple-element.12.low, f32[256,256]{1,0:T(8,128)} %get-tuple-element.13.r_first, f32[128,128]{1,0:T(8,128)} %get-tuple-element.14.r_top, f32[128,128]{1,0:T(8,128)} %get-tuple-element.15.i_top, ...), custom_call_target="tpu_custom_call" | custom-call | tf_op jit(solution)/shard_map/second_factor/pallas_call | solution.py:546

commit v3 on v2

--- a/solution.py
+++ b/solution.py
@@ -171,69 +171,45 @@
 
 TOTAL = N_LEAF * N_BLK
 STEPS = (-1, 1)
+ONE, TWO = 0, 1
 
 
 class Exchange:
-    def __init__(self, device, near, far, relay, near_to, far_to, sems):
-        self.near_to, self.far_to = near_to, far_to
-        self.direct, self.away, self.onward = [], [], []
-        self.one, self.two, self.from_one, self.from_two = [], [], [], []
-        self.between = (device >= 1) & (device < TOTAL - 1)
-        for u, step in enumerate(STEPS):
-            peer = lax.rem(device + step + TOTAL, TOTAL)
-            there = (lax.div(peer, N_LEAF), lax.rem(peer, N_LEAF))
-
-            def copy(kind, src, dst):
-                return pltpu.make_async_remote_copy(
-                    src_ref=src, dst_ref=dst, send_sem=sems.at[0, kind, u], recv_sem=sems.at[1, kind, u],
-                    device_id=there, device_id_type=MESH)
-
-            self.direct.append(copy(0, near[u], near_to[u]))
-            self.away.append(copy(1, far[u], relay.at[u]))
-            self.onward.append(copy(2, relay.at[u], far_to[u]))
-            self.one.append(self.within(device + step))
-            self.two.append(self.within(device + 2 * step))
-            self.from_one.append(self.within(device - step))
-            self.from_two.append(self.within(device - 2 * step))
+    def __init__(self, device, near, far, near_to, far_to, sems):
+        self.to = (near_to, far_to)
+        self.copies, self.sends, self.arrives, self.peers = ([], []), ([], []), ([], []), []
+        for kind, (src, dst) in enumerate(((near, near_to), (far, far_to))):
+            for u, step in enumerate(STEPS):
+                step = step * (kind + 1)
+                peer = lax.rem(device + step + TOTAL, TOTAL)
+                there = (lax.div(peer, N_LEAF), lax.rem(peer, N_LEAF))
+                self.copies[kind].append(pltpu.make_async_remote_copy(
+                    src_ref=src[u], dst_ref=dst[u], send_sem=sems.at[0, kind, u], recv_sem=sems.at[1, kind, u],
+                    device_id=there, device_id_type=MESH))
+                self.sends[kind].append(self.within(device + step))
+                self.arrives[kind].append(self.within(device - step))
+                self.peers.append((self.sends[kind][u], self.arrives[kind][u], there))
 
     def within(self, device):
         return (device >= 0) & (device < TOTAL)
 
-    def send_far(self):
+    def send(self, kind):
         for u in range(2):
-            pl.when(self.two[u])(self.away[u].start)
-
-    def send_near(self):
+            pl.when(self.sends[kind][u])(self.copies[kind][u].start)
+
+    def receive(self, kind):
         for u in range(2):
-            pl.when(self.one[u])(self.direct[u].start)
-
-    def forward(self):
-        for u in range(2):
-            @pl.when(self.between)
+            to = self.to[kind][u]
+            pl.when(self.arrives[kind][u])(self.copies[kind][u].wait_recv)
+
+            @pl.when(jnp.logical_not(self.arrives[kind][u]))
             def _():
-                self.away[u].wait_recv()
-                self.onward[u].start()
-
-    def receive(self, arrives, copy, to):
-        pl.when(arrives)(copy.wait_recv)
-
-        @pl.when(jnp.logical_not(arrives))
-        def _():
-            to[...] = jnp.zeros(to.shape, F32)
-
-    def receive_near(self):
-        for u in range(2):
-            self.receive(self.from_one[u], self.direct[u], self.near_to[u])
-
-    def receive_far(self):
-        for u in range(2):
-            self.receive(self.from_two[u], self.onward[u], self.far_to[u])
+                to[...] = jnp.zeros(to.shape, F32)
 
     def drain(self):
-        for u in range(2):
-            pl.when(self.two[u])(self.away[u].wait_send)
-            pl.when(self.one[u])(self.direct[u].wait_send)
-            pl.when(self.between)(self.onward[u].wait_send)
+        for kind in range(2):
+            for u in range(2):
+                pl.when(self.sends[kind][u])(self.copies[kind][u].wait_send)
 
 
 STORED = (512, 256, 384, 640)
@@ -242,7 +218,7 @@
 
 
 def main_kernel(scale, count, modes, stiffness, connect, send, bottom_out, low_out, rest_out, r_out, top_out, inv_out, q_out,
-                outgoing, table, relay, acc, incoming, relay_back, halo_sems, back_sems,
+                outgoing, table, acc, incoming, halo_sems, back_sems,
                 ext_hi, ext_lo, pick, place, taken, blocks, matrix_hi, matrix_lo, product, stiff, work, *sums):
     leaf, blk = lax.axis_index("leaf"), lax.axis_index("blk")
     device = blk * N_LEAF + leaf
@@ -254,18 +230,16 @@
     halo, back = [], []
     for h in range(2):
         halo.append(Exchange(
-            device, [outgoing.at[h, j] for j in NEAR_OUT], [outgoing.at[h, j] for j in FAR_OUT], relay.at[h],
+            device, [outgoing.at[h, j] for j in NEAR_OUT], [outgoing.at[h, j] for j in FAR_OUT],
             [rows_of(table, h, j) for j in NEAR_OUT], [rows_of(table, h, j) for j in FAR_OUT], halo_sems.at[h]))
         back.append(Exchange(
-            device, [rows_of(acc, h, j) for j in NEAR_BACK], [rows_of(acc, h, j) for j in FAR_BACK], relay_back.at[h],
+            device, [rows_of(acc, h, j) for j in NEAR_BACK], [rows_of(acc, h, j) for j in FAR_BACK],
             [incoming.at[h, j] for j in NEAR_BACK], [incoming.at[h, j] for j in FAR_BACK], back_sems.at[h]))
     greeted = N_LEAF + N_BLK - 2
-    for u, step in enumerate(STEPS):
-        peer = lax.rem(device + step + TOTAL, TOTAL)
-        there = (lax.div(peer, N_LEAF), lax.rem(peer, N_LEAF))
-        greeted = greeted + halo[0].from_one[u].astype(jnp.int32)
-
-        @pl.when(halo[0].one[u])
+    for sends, arrives, there in halo[0].peers:
+        greeted = greeted + arrives.astype(jnp.int32)
+
+        @pl.when(sends)
         def _():
             pl.semaphore_signal(barrier, inc=1, device_id=there, device_id_type=MESH)
 
@@ -286,8 +260,8 @@
 
     prepare(0)
     pl.semaphore_wait(barrier, greeted)
-    halo[0].send_far()
-    halo[0].send_near()
+    halo[0].send(TWO)
+    halo[0].send(ONE)
     prepare(1)
     gram = sum(dot3(modes[c].T, modes[c], 1, 0) for c in range(3))
     first.begin(gram[0:128, 0:128], gram[128:256, 0:128], gram[128:256, 128:256])
@@ -304,9 +278,8 @@
         pick[128 * k : 128 * (k + 1), :] = (columns[:, k : k + 1] == lanes).astype(BF16)
         place[:, 128 * k : 128 * (k + 1)] = (rows == conn[k : k + 1, :]).astype(BF16)
 
-    halo[0].forward()
-    halo[1].send_far()
-    halo[1].send_near()
+    halo[1].send(TWO)
+    halo[1].send(ONE)
 
     def gather(h, part):
         span = slice(256 * part, 256 * (part + 1))
@@ -372,29 +345,27 @@
 
     OWN, NEAR, FAR = slice(0, 256), slice(256, 512), slice(512, 768)
 
-    halo[0].receive_near()
+    halo[0].receive(ONE)
     gather(0, 1)
-    halo[0].receive_far()
+    halo[0].receive(TWO)
     gather(0, 2)
     halves = multiply(0)
     first.across()
     scatter(0, halves, FAR)
-    back[0].send_far()
-    halo[1].forward()
+    back[0].send(TWO)
     scatter(0, halves, NEAR)
-    back[0].send_near()
+    back[0].send(ONE)
     scatter(0, halves, OWN)
-    halo[1].receive_near()
+    halo[1].receive(ONE)
     gather(1, 1)
-    halo[1].receive_far()
+    halo[1].receive(TWO)
     gather(1, 2)
     first.gather()
     halves = multiply(1)
     scatter(1, halves, FAR)
-    back[1].send_far()
-    back[0].forward()
+    back[1].send(TWO)
     scatter(1, halves, NEAR)
-    back[1].send_near()
+    back[1].send(ONE)
     scatter(1, halves, OWN)
 
     lower, diagonal = [], 0.0
@@ -416,8 +387,8 @@
     to_own = jnp.concatenate([(rows == chosen[j : j + 1, :]).astype(BF16) for j in range(4)], axis=1)
 
     def complete(h):
-        back[h].receive_near()
-        back[h].receive_far()
+        back[h].receive(ONE)
+        back[h].receive(TWO)
         parts = split2(jnp.concatenate([incoming[h, j] for j in range(4)], axis=0))
         whole = acc[h, OWN, :] + sum(dot(to_own, part, 1, 0) for part in parts)
         for c in range(3):
@@ -426,7 +397,6 @@
     first.end()
     factor_start(work, first.total[0:128, :])
     factor(work, 0)
-    back[1].forward()
     factor(work, 64)
     r00, i00 = factored(work)
     complete(0)
@@ -486,15 +456,14 @@
     shapes = ((256, 128), (256, 256), (3, 256, 128), (256, 256), (128, 128), (128, 128), (3, 256, 384))
     rows = pltpu.VMEM((2, 4, 128, 384), F32)
     table = pltpu.VMEM((2, 768, 384), F32)
-    relay = pltpu.VMEM((2, 2, 128, 384), F32)
-    sems = pltpu.SemaphoreType.DMA((2, 2, 3, 2))
+    sems = pltpu.SemaphoreType.DMA((2, 2, 2, 2))
     return pl.pallas_call(
         functools.partial(main_kernel, scale),
         out_shape=[jax.ShapeDtypeStruct(shape, F32) for shape in shapes],
         in_specs=[SMEM] + [VMEM] * 4,
         out_specs=[VMEM] * len(shapes),
         scratch_shapes=[
-            rows, table, relay, table, rows, relay, sems, sems,
+            rows, table, table, rows, sems, sems,
             pltpu.VMEM((2, 768, 384), BF16),
             pltpu.VMEM((2, 768, 384), BF16),
             pltpu.VMEM((1280, 768), BF16),
@@ -512,16 +481,17 @@
     )(count, modes, stiffness, connect, send)
 
 
-def second_kernel(scale, bottom, low, r_first, r_top, i_top, rest, q_in, q_out, r_out, work, top_columns, last, sems):
-    done = pltpu.make_async_copy(q_in, q_out.at[:, :, pl.ds(0, 384)], sems.at[0])
-    fetch = pltpu.make_async_copy(q_in.at[:, :, pl.ds(256, 128)], top_columns, sems.at[1])
-    done.start()
+def second_kernel(scale, bottom, low, r_first, r_top, i_top, rest, q_in, q_out, r_out, work, columns, last, sems):
+    fetch = pltpu.make_async_copy(q_in, columns, sems.at[0])
+    done = pltpu.make_async_copy(columns, q_out.at[:, :, pl.ds(0, 384)], sems.at[1])
     fetch.start()
     low0, low1 = low[0:128, :], low[128:256, :]
     side = bottom[0:128, :] - dot(low1, low0, 1, 1, HIGH)
     r01 = dot(i_top[...], side, 1, 1, HIGH)
     factor_start(work, bottom[128:256, :] - dot(low1, low1, 1, 1, HIGH) - dot(r01, r01, 0, 0, HIGH))
     factor(work, 0)
+    fetch.wait()
+    done.start()
     r_out[0:256, 0:256] = r_first[...] / scale
     r_out[0:256, 256:512] = low[...].T / scale
     r_out[256:512, 0:256] = jnp.zeros((256, 256), F32)
@@ -531,9 +501,8 @@
     factor(work, 64)
     r11, i11 = factored(work)
     r_out[384:512, 384:512] = r11 / scale
-    fetch.wait()
     for c in range(3):
-        left = rest[c] - dot3(top_columns[c], r01 / scale, 1, 0)
+        left = rest[c] - dot3(columns[c, :, 256:384], r01 / scale, 1, 0)
         last[c] = dot3(left, i11, 1, 1) * scale
     place = pltpu.make_async_copy(last, q_out.at[:, :, pl.ds(384, 128)], sems.at[2])
     place.start()
@@ -550,7 +519,7 @@
         out_specs=[anywhere, VMEM],
         scratch_shapes=[
             pltpu.VMEM((SIDE, 2 * SIDE), F32),
-            pltpu.VMEM((3, 256, 128), F32),
+            pltpu.VMEM((3, 256, 384), F32),
             pltpu.VMEM((3, 256, 128), F32),
             pltpu.SemaphoreType.DMA((3,)),
         ],

time: 141 us -> 117 us (0.83)
  Pallas kernels: 139 us -> 115 us
    pallas_call x1, Pallas kernels: 39.1 us -> 8.2 us  [second(): pl.pallas_call(functools.partial(second_kernel, scale), out_shape=[jax.Sh...]
    pallas_call x1, Pallas kernels: 99.8 us -> 107 us  [up_to_last_gram(): pl.pallas_call(functools.partial(main_kernel, scale), out_shape=[jax.Shap...]
where the time goes in v3:
time: 117 us
  Pallas kernels  115 us (98%)
  between operations  1.47 us (1%)
    pallas_call x1, Pallas kernels, up_to_last_gram(): pl.pallas_call(functools.partial(main_kernel, scale), out_shape=[jax.Shap...  107 us
    pallas_call x1, Pallas kernels, second(): pl.pallas_call(functools.partial(second_kernel, scale), out_shape=[jax.Sh...  8.2 us

profile of v3, /device:TPU:0, one launch (start us, length us, event | category | flops | bytes accessed | tf_op | source)
XLA Modules:
  0.0 116.7 jit_solution(5014797694335496675)
XLA Ops:
  1.3 107.1 %up_to_last_gram.1 = (f32[256,128]{1,0:T(8,128)}, f32[256,256]{1,0:T(8,128)}, f32[3,256,128]{2,1,0:T(8,128)}, f32[256,256]{1,0:T(8,128)}, f32[128,128]{1,0:T(8,1...) custom-call(s32[1]{0:T(128)S(6)} %copy.7.count, f32[3,256,256]{2,1,0:T(8,128)} %bitcast.3, ...), custom_call_target="tpu_custom_call" | custom-call | tf_op jit(solution)/shard_map/up_to_last_gram/pallas_call | solution.py:460
  108.3 8.2 %second_factor.1 = (f32[3,256,512]{2,1,0:T(8,128)}, f32[512,512]{1,0:T(8,128)}) custom-call(f32[256,128]{1,0:T(8,128)} %get-tuple-element.11.bottom, f32[256,256]{1,0:T(8,128)} %get-tuple-element.12.low, f32[256,256]{1,0:T(8,128)} %get-tuple-element.13.r_first, f32[128,128]{1,0:T(8,128)} %get-tuple-element.14.r_top, f32[128,128]{1,0:T(8,128)} %get-tuple-element.15.i_top, ...), custom_call_target="tpu_custom_call" | custom-call | tf_op jit(solution)/shard_map/second_factor/pallas_call | solution.py:515

commit v4 on v2

--- a/solution.py
+++ b/solution.py
@@ -114,6 +114,99 @@
         pltpu.VMEM((N_BLK, size, 128), F32),
         pltpu.VMEM((128 * parts, 128), F32),
         pltpu.SemaphoreType.DMA((4, N_LEAF)),
+        pltpu.SemaphoreType.DMA((2, N_BLK)),
+    ]
+
+
+CHUNK = 24
+
+
+class AxisSum:
+    def __init__(self, leaf, blk, local, along_x, part, along_y, far, total, sems, blk_sems):
+        self.blk, self.local, self.part, self.total = blk, local, part, total
+        self.along_x, self.along_y, self.far = along_x, along_y, far
+        x, y = lax.div(leaf, 4), lax.rem(leaf, 4)
+        wide, slim = 4 * CHUNK, CHUNK
+        self.wide = pl.ds(pl.multiple_of(x * wide, 8), wide)
+        self.slim = pl.ds(pl.multiple_of(y * slim, 8), slim)
+        self.mine = pl.ds(pl.multiple_of(leaf * slim, 8), slim)
+        self.stages = [[], [], [], [], []]
+
+        def copy(stage, k, src, dst, sem, peer):
+            self.stages[stage].append(pltpu.make_async_remote_copy(
+                src_ref=src, dst_ref=dst, send_sem=sem.at[0, k], recv_sem=sem.at[1, k],
+                device_id=peer, device_id_type=MESH))
+
+        for k in range(1, 4):
+            px, py = lax.rem(x + k, 4), lax.rem(y + k, 4)
+            beside, above = {"leaf": px * 4 + y}, {"leaf": x * 4 + py}
+            copy(0, k, local.at[pl.ds(pl.multiple_of(px * wide, 8), wide)], along_x.at[k], sems.at[0], beside)
+            copy(1, k, part.at[pl.ds(pl.multiple_of(py * slim, 8), slim)], along_y.at[k], sems.at[1], above)
+            copy(3, k, total.at[self.mine], total.at[self.mine], sems.at[2], above)
+            copy(4, k, total.at[self.wide], total.at[self.wide], sems.at[3], beside)
+        for k in range(1, N_BLK):
+            copy(2, k, far.at[blk], far.at[blk], blk_sems, {"blk": lax.rem(blk + k, N_BLK)})
+
+    def start(self, stage):
+        for copy in self.stages[stage]:
+            copy.start()
+
+    def wait(self, stage):
+        for copy in self.stages[stage]:
+            copy.wait_recv()
+
+    def begin(self, gram):
+        self.local[0:128, :] = gram[0:128, 0:128]
+        self.local[128:256, :] = gram[128:256, 0:128]
+        self.local[256:384, :] = gram[128:256, 128:256]
+        self.start(0)
+
+    def second(self):
+        self.wait(0)
+        part = self.local[self.wide, :]
+        for k in range(1, 4):
+            part = part + self.along_x[k]
+        self.part[...] = part
+        self.start(1)
+
+    def third(self):
+        self.wait(1)
+        part = self.part[self.slim, :]
+        for k in range(1, 4):
+            part = part + self.along_y[k]
+        self.far[self.blk] = part
+        self.start(2)
+
+    def fourth(self):
+        self.wait(2)
+        part = self.far[0]
+        for b in range(1, N_BLK):
+            part = part + self.far[b]
+        self.total[self.mine, :] = part
+        self.start(3)
+
+    def fifth(self):
+        self.wait(3)
+        self.start(4)
+
+    def end(self):
+        self.wait(4)
+
+    def drain(self):
+        for stage in self.stages:
+            for copy in stage:
+                copy.wait_send()
+
+
+def axis_sum_scratch():
+    return [
+        pltpu.VMEM((384, 128), F32),
+        pltpu.VMEM((4, 4 * CHUNK, 128), F32),
+        pltpu.VMEM((4 * CHUNK, 128), F32),
+        pltpu.VMEM((4, CHUNK, 128), F32),
+        pltpu.VMEM((N_BLK, CHUNK, 128), F32),
+        pltpu.VMEM((384, 128), F32),
+        pltpu.SemaphoreType.DMA((4, 2, 4)),
         pltpu.SemaphoreType.DMA((2, N_BLK)),
     ]
 
@@ -199,13 +292,11 @@
     def within(self, device):
         return (device >= 0) & (device < TOTAL)
 
-    def send_far(self):
-        for u in range(2):
-            pl.when(self.two[u])(self.away[u].start)
-
-    def send_near(self):
-        for u in range(2):
-            pl.when(self.one[u])(self.direct[u].start)
+    def send_far(self, u):
+        pl.when(self.two[u])(self.away[u].start)
+
+    def send_near(self, u):
+        pl.when(self.one[u])(self.direct[u].start)
 
     def forward(self):
         for u in range(2):
@@ -239,6 +330,8 @@
 STORED = (512, 256, 384, 640)
 NEAR_OUT, FAR_OUT = (1, 2), (0, 3)
 NEAR_BACK, FAR_BACK = (2, 1), (3, 0)
+OWN, NEAR, FAR = slice(0, 256), slice(256, 512), slice(512, 768)
+COMPONENTS = [slice(256 * c, 256 * (c + 1)) for c in range(3)]
 
 
 def main_kernel(scale, count, modes, stiffness, connect, send, bottom_out, low_out, rest_out, r_out, top_out, inv_out, q_out,
@@ -248,49 +341,49 @@
     device = blk * N_LEAF + leaf
     barrier = greet(leaf, blk)
 
-    def rows_of(ref, h, j):
-        return ref.at[h, pl.ds(STORED[j], 128)]
-
-    halo, back = [], []
-    for h in range(2):
-        halo.append(Exchange(
-            device, [outgoing.at[h, j] for j in NEAR_OUT], [outgoing.at[h, j] for j in FAR_OUT], relay.at[h],
-            [rows_of(table, h, j) for j in NEAR_OUT], [rows_of(table, h, j) for j in FAR_OUT], halo_sems.at[h]))
-        back.append(Exchange(
-            device, [rows_of(acc, h, j) for j in NEAR_BACK], [rows_of(acc, h, j) for j in FAR_BACK], relay_back.at[h],
-            [incoming.at[h, j] for j in NEAR_BACK], [incoming.at[h, j] for j in FAR_BACK], back_sems.at[h]))
+    def rows_of(ref, j):
+        return ref.at[pl.ds(STORED[j], 128)]
+
+    halo = Exchange(
+        device, [outgoing.at[j] for j in NEAR_OUT], [outgoing.at[j] for j in FAR_OUT], relay,
+        [rows_of(table, j) for j in NEAR_OUT], [rows_of(table, j) for j in FAR_OUT], halo_sems)
+    back = Exchange(
+        device, [rows_of(acc, j) for j in NEAR_BACK], [rows_of(acc, j) for j in FAR_BACK], relay_back,
+        [incoming.at[j] for j in NEAR_BACK], [incoming.at[j] for j in FAR_BACK], back_sems)
     greeted = N_LEAF + N_BLK - 2
     for u, step in enumerate(STEPS):
         peer = lax.rem(device + step + TOTAL, TOTAL)
         there = (lax.div(peer, N_LEAF), lax.rem(peer, N_LEAF))
-        greeted = greeted + halo[0].from_one[u].astype(jnp.int32)
-
-        @pl.when(halo[0].one[u])
+        greeted = greeted + halo.from_one[u].astype(jnp.int32)
+
+        @pl.when(halo.one[u])
         def _():
             pl.semaphore_signal(barrier, inc=1, device_id=there, device_id_type=MESH)
 
-    first, cross, top, bottom = (Sum(leaf, blk, *sums[6 * i : 6 * i + 6]) for i in range(4))
+    first, cross = (AxisSum(leaf, blk, *sums[8 * i : 8 * i + 8]) for i in range(2))
+    top, bottom = (Sum(leaf, blk, *sums[16 + 6 * i : 22 + 6 * i]) for i in range(2))
 
     chosen = send[...]
     columns = columns_of(chosen, 4)
     nodes = lax.broadcasted_iota(jnp.int32, (128, 256), 1).astype(F32)
-    choosers = [(columns[:, j : j + 1] == nodes).astype(BF16) for j in range(4)]
-
-    def prepare(h):
-        wide = jnp.concatenate([modes[c, :, 128 * h : 128 * (h + 1)] for c in range(3)], axis=1)
-        parts = split3(wide)
-        for j in FAR_OUT + NEAR_OUT:
-            outgoing[h, j] = sum(dot(choosers[j], part, 1, 0) for part in parts)
-        table[h, 0:256, :] = wide
-        ext_hi[h, 0:256, :], ext_lo[h, 0:256, :] = parts[0], parts[1]
-
-    prepare(0)
+    wide = jnp.concatenate([modes[c] for c in range(3)], axis=1)
+    parts = split3(wide)
+
+    def prepare(j):
+        chooser = (columns[:, j : j + 1] == nodes).astype(BF16)
+        outgoing[j] = sum(dot(chooser, part, 1, 0) for part in parts)
+
+    prepare(FAR_OUT[0])
     pl.semaphore_wait(barrier, greeted)
-    halo[0].send_far()
-    halo[0].send_near()
-    prepare(1)
-    gram = sum(dot3(modes[c].T, modes[c], 1, 0) for c in range(3))
-    first.begin(gram[0:128, 0:128], gram[128:256, 0:128], gram[128:256, 128:256])
+    halo.send_far(0)
+    prepare(FAR_OUT[1])
+    halo.send_far(1)
+    for u in range(2):
+        prepare(NEAR_OUT[u])
+        halo.send_near(u)
+    table[OWN, :] = wide
+    ext_hi[OWN, :], ext_lo[OWN, :] = parts[0], parts[1]
+    first.begin(sum(dot3(modes[c].T, modes[c], 1, 0) for c in range(3)))
 
     conn = connect[...]
     columns = columns_of(conn, 10)
@@ -304,26 +397,20 @@
         pick[128 * k : 128 * (k + 1), :] = (columns[:, k : k + 1] == lanes).astype(BF16)
         place[:, 128 * k : 128 * (k + 1)] = (rows == conn[k : k + 1, :]).astype(BF16)
 
-    halo[0].forward()
-    halo[1].send_far()
-    halo[1].send_near()
-
-    def gather(h, part):
-        span = slice(256 * part, 256 * (part + 1))
-        if part:
-            ext_hi[h, span, :], ext_lo[h, span, :] = split2(table[h, span, :])
+    def gather(span):
+        if span is not OWN:
+            ext_hi[span, :], ext_lo[span, :] = split2(table[span, :])
 
         def body(step, carry):
             at = pl.ds(pl.multiple_of(step * 320, 320), 320)
             picked = pick[at, span]
-            found = dot(picked, ext_hi[h, span, :], 1, 0) + dot(picked, ext_lo[h, span, :], 1, 0)
-            taken[h, at, :] = found if part == 0 else taken[h, at, :] + found
+            found = dot(picked, ext_hi[span, :], 1, 0) + dot(picked, ext_lo[span, :], 1, 0)
+            taken[at, :] = found if span is OWN else taken[at, :] + found
             return carry
 
         lax.fori_loop(0, 4, body, 0)
 
-    gather(0, 0)
-    gather(1, 0)
+    gather(OWN)
 
     live = lax.broadcasted_iota(jnp.int32, (30, 128), 1) < count[0]
     source = lax.broadcasted_iota(jnp.int32, (30, 256), 0)
@@ -336,6 +423,7 @@
             hi, lo = split2(jnp.where(live, block, 0.0))
             blocks[10 * c + k] = dot(hi, spread, 0, 0) + dot(lo, spread, 0, 0)
 
+    halo.forward()
     keep = lax.broadcasted_iota(jnp.int32, (8, 256), 0) == lax.rem(lax.broadcasted_iota(jnp.int32, (8, 256), 1), 8)
 
     def assemble(g, carry):
@@ -345,112 +433,86 @@
         return carry
 
     lax.fori_loop(0, 16, assemble, 0)
-
-    def multiply(h):
-        def group(g, carry):
-            spans = [pl.ds(pl.multiple_of(128 * k + g * 8, 8), 8) for k in range(10)]
-            vectors = jnp.concatenate(
-                [taken[h, spans[l], 128 * d : 128 * (d + 1)] for d in range(3) for l in range(10)]
-                + [jnp.zeros((16, 128), F32)],
-                axis=0,
-            )
-            v_hi, v_lo = split2(vectors)
-            m_hi, m_lo = matrix_hi[g], matrix_lo[g]
-            result = dot(m_hi, v_hi, 1, 0) + (dot(m_hi, v_lo, 1, 0) + dot(m_lo, v_hi, 1, 0))
-            for c in range(3):
-                for k in range(10):
-                    n = 10 * c + k
-                    product[spans[k], 128 * c : 128 * (c + 1)] = result[8 * n : 8 * n + 8, :]
-            return carry
-
-        lax.fori_loop(0, 16, group, 0, unroll=2)
-        return split2(product[...])
-
-    def scatter(h, halves, span):
+    halo.receive_near()
+    gather(NEAR)
+    first.second()
+    halo.receive_far()
+    first.third()
+    gather(FAR)
+    first.fourth()
+
+    def group(g, carry):
+        spans = [pl.ds(pl.multiple_of(128 * k + g * 8, 8), 8) for k in range(10)]
+        vectors = jnp.concatenate(
+            [taken[spans[l], COMPONENTS[d]] for d in range(3) for l in range(10)] + [jnp.zeros((16, 256), F32)], axis=0)
+        v_hi, v_lo = split2(vectors)
+        m_hi, m_lo = matrix_hi[g], matrix_lo[g]
+        result = dot(m_hi, v_hi, 1, 0) + (dot(m_hi, v_lo, 1, 0) + dot(m_lo, v_hi, 1, 0))
+        for c in range(3):
+            for k in range(10):
+                n = 10 * c + k
+                product[spans[k], COMPONENTS[c]] = result[8 * n : 8 * n + 8, :]
+        return carry
+
+    lax.fori_loop(0, 16, group, 0, unroll=2)
+    first.fifth()
+    halves = [split2(product[:, at]) for at in COMPONENTS]
+
+    def scatter(span):
         where = place[span, :]
-        acc[h, span, :] = dot(where, halves[0], 1, 0) + dot(where, halves[1], 1, 0)
-
-    OWN, NEAR, FAR = slice(0, 256), slice(256, 512), slice(512, 768)
-
-    halo[0].receive_near()
-    gather(0, 1)
-    halo[0].receive_far()
-    gather(0, 2)
-    halves = multiply(0)
-    first.across()
-    scatter(0, halves, FAR)
-    back[0].send_far()
-    halo[1].forward()
-    scatter(0, halves, NEAR)
-    back[0].send_near()
-    scatter(0, halves, OWN)
-    halo[1].receive_near()
-    gather(1, 1)
-    halo[1].receive_far()
-    gather(1, 2)
-    first.gather()
-    halves = multiply(1)
-    scatter(1, halves, FAR)
-    back[1].send_far()
-    back[0].forward()
-    scatter(1, halves, NEAR)
-    back[1].send_near()
-    scatter(1, halves, OWN)
-
-    lower, diagonal = [], 0.0
-    for c in range(3):
-        at = slice(128 * c, 128 * (c + 1))
-        tables = [jnp.concatenate([ext[0, :, at], ext[1, :, at]], axis=1) for ext in (ext_hi, ext_lo)]
-        for h in range(2):
-            hi, lo = split2(acc[h, :, at].T)
-            t_hi, t_lo = (t if h else t[:, 0:128] for t in tables)
-            found = dot(hi, t_hi, 1, 0) + (dot(hi, t_lo, 1, 0) + dot(lo, t_hi, 1, 0))
-            if h:
-                lower.append(found)
-            else:
-                diagonal = diagonal + found
-    lower = sum(lower)
-    cross.begin(diagonal, lower[:, 0:128], lower[:, 128:256])
-
-    rows = lax.broadcasted_iota(jnp.int32, (256, 128), 0)
-    to_own = jnp.concatenate([(rows == chosen[j : j + 1, :]).astype(BF16) for j in range(4)], axis=1)
-
-    def complete(h):
-        back[h].receive_near()
-        back[h].receive_far()
-        parts = split2(jnp.concatenate([incoming[h, j] for j in range(4)], axis=0))
-        whole = acc[h, OWN, :] + sum(dot(to_own, part, 1, 0) for part in parts)
-        for c in range(3):
-            stiff[c, :, 128 * h : 128 * (h + 1)] = whole[:, 128 * c : 128 * (c + 1)]
+        for c, at in enumerate(COMPONENTS):
+            acc[span, at] = dot(where, halves[c][0], 1, 0) + dot(where, halves[c][1], 1, 0)
+
+    scatter(FAR)
+    back.send_far(0)
+    back.send_far(1)
+    scatter(NEAR)
+    back.send_near(0)
+    back.send_near(1)
+    scatter(OWN)
+
+    gram = jnp.zeros((256, 256), F32)
+    for at in COMPONENTS:
+        hi, lo = split2(acc[:, at].T)
+        t_hi, t_lo = ext_hi[:, at], ext_lo[:, at]
+        gram = gram + (dot(hi, t_hi, 1, 0) + (dot(hi, t_lo, 1, 0) + dot(lo, t_hi, 1, 0)))
+    cross.begin(gram)
 
     first.end()
     factor_start(work, first.total[0:128, :])
     factor(work, 0)
-    back[1].forward()
     factor(work, 64)
+    back.forward()
     r00, i00 = factored(work)
-    complete(0)
-    top.begin(sum(dot3(stiff[c, :, 0:128].T, stiff[c, :, 0:128], 1, 0) for c in range(3)))
     r01 = dot(i00, first.total[128:256, :], 1, 1, HIGH)
     factor_start(work, first.total[256:384, :] - dot(r01, r01, 0, 0, HIGH))
     factor(work, 0)
     factor(work, 64)
     r11, i11 = factored(work)
+    cross.second()
     r_out[0:128, 0:128], r_out[0:128, 128:256] = r00, r01
     r_out[128:256, 0:128], r_out[128:256, 128:256] = jnp.zeros((SIDE, SIDE), F32), r11
     i10 = dot(i11, dot(r01, i00, 0, 0, HIGH), 1, 0, HIGH)
     inv = jnp.concatenate(
         [jnp.concatenate([i00, jnp.zeros((SIDE, SIDE), F32)], axis=1), jnp.concatenate([-i10, i11], axis=1)], axis=0)
-    cross.across()
     for c in range(3):
         q_out[c, :, 0:256] = dot3(modes[c], inv, 1, 1) * scale
-
-    complete(1)
-    both = sum(dot3(stiff[c, :, 128:256].T, stiff[c], 1, 0) for c in range(3))
-    bottom.begin(both[:, 0:128], both[:, 128:256])
-    cross.gather()
-    top.across()
-    top.gather()
+    cross.third()
+
+    rows = lax.broadcasted_iota(jnp.int32, (256, 128), 0)
+    to_own = jnp.concatenate([(rows == chosen[j : j + 1, :]).astype(BF16) for j in range(4)], axis=1)
+    back.receive_near()
+    cross.fourth()
+    back.receive_far()
+    cross.fifth()
+    gram = jnp.zeros((256, 256), F32)
+    for c, at in enumerate(COMPONENTS):
+        halves = split2(jnp.concatenate([incoming[j, :, at] for j in range(4)], axis=0))
+        whole = acc[OWN, at] + sum(dot(to_own, half, 1, 0) for half in halves)
+        stiff[c] = whole
+        gram = gram + dot3(whole.T, whole, 1, 0)
+    top.begin(gram[0:128, 0:128])
+    bottom.begin(gram[128:256, 0:128], gram[128:256, 128:256])
     cross.end()
     crossed = cross.total
     gram = jnp.concatenate(
@@ -458,24 +520,26 @@
          jnp.concatenate([crossed[128:256, :], crossed[256:384, :]], axis=1)], axis=0)
     low = dot(gram, inv, 1, 1, HIGH)
     low_out[...] = low
+    top.across()
+    bottom.across()
+    for c in range(3):
+        stiff[c] = stiff[c] - dot3(q_out[c, :, 0:256], low / scale, 1, 1)
+    top.gather()
+    bottom.gather()
+    halo.drain()
+    back.drain()
+    first.drain()
+    cross.drain()
     top.end()
     factor_start(work, top.total[...] - dot(low[0:128, :], low[0:128, :], 1, 1, HIGH))
     factor(work, 0)
-    bottom.across()
     factor(work, 64)
-    bottom.gather()
     r22, i22 = factored(work)
     top_out[...] = r22
     inv_out[...] = i22
     for c in range(3):
-        rest = stiff[c] - dot3(q_out[c, :, 0:256], low / scale, 1, 1)
-        q_out[c, :, 256:384] = dot3(rest[:, 0:128], i22, 1, 1) * scale
-        rest_out[c] = rest[:, 128:256]
-    for h in range(2):
-        halo[h].drain()
-        back[h].drain()
-    first.drain()
-    cross.drain()
+        q_out[c, :, 256:384] = dot3(stiff[c, :, 0:128], i22, 1, 1) * scale
+        rest_out[c] = stiff[c, :, 128:256]
     top.drain()
     bottom.end()
     bottom.drain()
@@ -484,10 +548,10 @@
 
 def up_to_last_gram(scale, count, modes, stiffness, connect, send):
     shapes = ((256, 128), (256, 256), (3, 256, 128), (256, 256), (128, 128), (128, 128), (3, 256, 384))
-    rows = pltpu.VMEM((2, 4, 128, 384), F32)
-    table = pltpu.VMEM((2, 768, 384), F32)
-    relay = pltpu.VMEM((2, 2, 128, 384), F32)
-    sems = pltpu.SemaphoreType.DMA((2, 2, 3, 2))
+    rows = pltpu.VMEM((4, 128, 768), F32)
+    table = pltpu.VMEM((768, 768), F32)
+    relay = pltpu.VMEM((2, 128, 768), F32)
+    sems = pltpu.SemaphoreType.DMA((2, 3, 2))
     return pl.pallas_call(
         functools.partial(main_kernel, scale),
         out_shape=[jax.ShapeDtypeStruct(shape, F32) for shape in shapes],
@@ -495,33 +559,34 @@
         out_specs=[VMEM] * len(shapes),
         scratch_shapes=[
             rows, table, relay, table, rows, relay, sems, sems,
-            pltpu.VMEM((2, 768, 384), BF16),
-            pltpu.VMEM((2, 768, 384), BF16),
+            pltpu.VMEM((768, 768), BF16),
+            pltpu.VMEM((768, 768), BF16),
             pltpu.VMEM((1280, 768), BF16),
             pltpu.VMEM((768, 1280), BF16),
-            pltpu.VMEM((2, 1280, 384), F32),
+            pltpu.VMEM((1280, 768), F32),
             pltpu.VMEM((30, 128, 256), F32),
             pltpu.VMEM((16, 240, 256), BF16),
             pltpu.VMEM((16, 240, 256), BF16),
-            pltpu.VMEM((1280, 384), F32),
+            pltpu.VMEM((1280, 768), F32),
             pltpu.VMEM((3, 256, 256), F32),
             pltpu.VMEM((SIDE, 2 * SIDE), F32),
-        ] + sum_scratch(3) + sum_scratch(3) + sum_scratch(1) + sum_scratch(2),
+        ] + axis_sum_scratch() + axis_sum_scratch() + sum_scratch(1) + sum_scratch(2),
         compiler_params=pltpu.CompilerParams(collective_id=1, has_side_effects=True, vmem_limit_bytes=LIMIT),
         name="up_to_last_gram",
     )(count, modes, stiffness, connect, send)
 
 
-def second_kernel(scale, bottom, low, r_first, r_top, i_top, rest, q_in, q_out, r_out, work, top_columns, last, sems):
-    done = pltpu.make_async_copy(q_in, q_out.at[:, :, pl.ds(0, 384)], sems.at[0])
-    fetch = pltpu.make_async_copy(q_in.at[:, :, pl.ds(256, 128)], top_columns, sems.at[1])
-    done.start()
+def second_kernel(scale, bottom, low, r_first, r_top, i_top, rest, q_in, q_out, r_out, work, columns, last, sems):
+    fetch = pltpu.make_async_copy(q_in, columns, sems.at[0])
+    done = pltpu.make_async_copy(columns, q_out.at[:, :, pl.ds(0, 384)], sems.at[1])
     fetch.start()
     low0, low1 = low[0:128, :], low[128:256, :]
     side = bottom[0:128, :] - dot(low1, low0, 1, 1, HIGH)
     r01 = dot(i_top[...], side, 1, 1, HIGH)
     factor_start(work, bottom[128:256, :] - dot(low1, low1, 1, 1, HIGH) - dot(r01, r01, 0, 0, HIGH))
     factor(work, 0)
+    fetch.wait()
+    done.start()
     r_out[0:256, 0:256] = r_first[...] / scale
     r_out[0:256, 256:512] = low[...].T / scale
     r_out[256:512, 0:256] = jnp.zeros((256, 256), F32)
@@ -531,9 +596,8 @@
     factor(work, 64)
     r11, i11 = factored(work)
     r_out[384:512, 384:512] = r11 / scale
-    fetch.wait()
     for c in range(3):
-        left = rest[c] - dot3(top_columns[c], r01 / scale, 1, 0)
+        left = rest[c] - dot3(columns[c, :, 256:384], r01 / scale, 1, 0)
         last[c] = dot3(left, i11, 1, 1) * scale
     place = pltpu.make_async_copy(last, q_out.at[:, :, pl.ds(384, 128)], sems.at[2])
     place.start()
@@ -550,7 +614,7 @@
         out_specs=[anywhere, VMEM],
         scratch_shapes=[
             pltpu.VMEM((SIDE, 2 * SIDE), F32),
-            pltpu.VMEM((3, 256, 128), F32),
+            pltpu.VMEM((3, 256, 384), F32),
             pltpu.VMEM((3, 256, 128), F32),
             pltpu.SemaphoreType.DMA((3,)),
         ],

time: 141 us -> 122 us (0.87)
  Pallas kernels: 139 us -> 120 us
    pallas_call x1, Pallas kernels: 39.1 us -> 8.2 us  [second(): pl.pallas_call(functools.partial(second_kernel, scale), out_shape=[jax.Sh...]
    pallas_call x1, Pallas kernels: 99.8 us -> 112 us  [up_to_last_gram(): pl.pallas_call(functools.partial(main_kernel, scale), out_shape=[jax.Shap...]
where the time goes in v4:
time: 122 us
  Pallas kernels  120 us (98%)
  between operations  1.47 us (1%)
    pallas_call x1, Pallas kernels, up_to_last_gram(): pl.pallas_call(functools.partial(main_kernel, scale), out_shape=[jax.Shap...  112 us
    pallas_call x1, Pallas kernels, second(): pl.pallas_call(functools.partial(second_kernel, scale), out_shape=[jax.Sh...  8.2 us

profile of v4, /device:TPU:0, one launch (start us, length us, event | category | flops | bytes accessed | tf_op | source)
XLA Modules:
  0.0 121.5 jit_solution(15291877950711255509)
XLA Ops:
  1.3 111.8 %up_to_last_gram.1 = (f32[256,128]{1,0:T(8,128)}, f32[256,256]{1,0:T(8,128)}, f32[3,256,128]{2,1,0:T(8,128)}, f32[256,256]{1,0:T(8,128)}, f32[128,128]{1,0:T(8,1...) custom-call(s32[1]{0:T(128)S(6)} %copy.7.count, f32[3,256,256]{2,1,0:T(8,128)} %bitcast.3, ...), custom_call_target="tpu_custom_call" | custom-call | tf_op jit(solution)/shard_map/up_to_last_gram/pallas_call | solution.py:555
  113.1 8.2 %second_factor.1 = (f32[3,256,512]{2,1,0:T(8,128)}, f32[512,512]{1,0:T(8,128)}) custom-call(f32[256,128]{1,0:T(8,128)} %get-tuple-element.11.bottom, f32[256,256]{1,0:T(8,128)} %get-tuple-element.12.low, f32[256,256]{1,0:T(8,128)} %get-tuple-element.13.r_first, f32[128,128]{1,0:T(8,128)} %get-tuple-element.14.r_top, f32[128,128]{1,0:T(8,128)} %get-tuple-element.15.i_top, ...), custom_call_target="tpu_custom_call" | custom-call | tf_op jit(solution)/shard_map/second_factor/pallas_call | solution.py:610

commit v5 on v2

--- a/solution.py
+++ b/solution.py
@@ -115,6 +115,86 @@
         pltpu.VMEM((128 * parts, 128), F32),
         pltpu.SemaphoreType.DMA((4, N_LEAF)),
         pltpu.SemaphoreType.DMA((2, N_BLK)),
+    ]
+
+
+class BlkSum:
+    def __init__(self, leaf, blk, local, along_blk, along_y, along_x, total, sems, blk_sems):
+        size = local.shape[0] // N_BLK
+        x, y = lax.div(leaf, 4), lax.rem(leaf, 4)
+        self.x, self.y, self.local, self.total = x, y, local, total
+        self.along_blk, self.along_y, self.along_x = along_blk, along_y, along_x
+        self.mine = pl.ds(pl.multiple_of(blk * size, 8), size)
+        self.stages = [[], [], [], []]
+
+        def copy(stage, k, src, dst, sem, peer):
+            self.stages[stage].append(pltpu.make_async_remote_copy(
+                src_ref=src, dst_ref=dst, send_sem=sem.at[0, k], recv_sem=sem.at[1, k],
+                device_id=peer, device_id_type=MESH))
+
+        for k in range(1, N_BLK):
+            peer = lax.rem(blk + k, N_BLK)
+            copy(0, k, local.at[pl.ds(pl.multiple_of(peer * size, 8), size)], along_blk.at[k], blk_sems.at[0], {"blk": peer})
+            copy(3, k, total.at[self.mine], total.at[self.mine], blk_sems.at[1], {"blk": peer})
+        for k in range(1, 4):
+            copy(1, k, along_y.at[y], along_y.at[y], sems.at[0], {"leaf": x * 4 + lax.rem(y + k, 4)})
+            copy(2, k, along_x.at[x], along_x.at[x], sems.at[1], {"leaf": lax.rem(x + k, 4) * 4 + y})
+
+    def start(self, stage):
+        for copy in self.stages[stage]:
+            copy.start()
+
+    def wait(self, stage):
+        for copy in self.stages[stage]:
+            copy.wait_recv()
+
+    def begin(self, *parts):
+        for n, part in enumerate(parts):
+            self.local[128 * n : 128 * (n + 1), :] = part
+        self.start(0)
+
+    def second(self):
+        self.wait(0)
+        part = self.local[self.mine, :]
+        for k in range(1, N_BLK):
+            part = part + self.along_blk[k]
+        self.along_y[self.y] = part
+        self.start(1)
+
+    def third(self):
+        self.wait(1)
+        part = self.along_y[0]
+        for k in range(1, 4):
+            part = part + self.along_y[k]
+        self.along_x[self.x] = part
+        self.start(2)
+
+    def fourth(self):
+        self.wait(2)
+        part = self.along_x[0]
+        for k in range(1, 4):
+            part = part + self.along_x[k]
+        self.total[self.mine, :] = part
+        self.start(3)
+
+    def end(self):
+        self.wait(3)
+
+    def drain(self):
+        for stage in self.stages:
+            for copy in stage:
+                copy.wait_send()
+
+
+def blk_sum_scratch():
+    return [
+        pltpu.VMEM((384, 128), F32),
+        pltpu.VMEM((N_BLK, 48, 128), F32),
+        pltpu.VMEM((4, 48, 128), F32),
+        pltpu.VMEM((4, 48, 128), F32),
+        pltpu.VMEM((384, 128), F32),
+        pltpu.SemaphoreType.DMA((2, 2, 4)),
+        pltpu.SemaphoreType.DMA((2, 2, N_BLK)),
     ]
 
 
@@ -269,28 +349,32 @@
         def _():
             pl.semaphore_signal(barrier, inc=1, device_id=there, device_id_type=MESH)
 
-    first, cross, top, bottom = (Sum(leaf, blk, *sums[6 * i : 6 * i + 6]) for i in range(4))
+    first, cross = (BlkSum(leaf, blk, *sums[7 * i : 7 * i + 7]) for i in range(2))
+    top, bottom = (Sum(leaf, blk, *sums[14 + 6 * i : 20 + 6 * i]) for i in range(2))
 
     chosen = send[...]
     columns = columns_of(chosen, 4)
     nodes = lax.broadcasted_iota(jnp.int32, (128, 256), 1).astype(F32)
     choosers = [(columns[:, j : j + 1] == nodes).astype(BF16) for j in range(4)]
 
-    def prepare(h):
-        wide = jnp.concatenate([modes[c, :, 128 * h : 128 * (h + 1)] for c in range(3)], axis=1)
-        parts = split3(wide)
-        for j in FAR_OUT + NEAR_OUT:
-            outgoing[h, j] = sum(dot(choosers[j], part, 1, 0) for part in parts)
-        table[h, 0:256, :] = wide
-        ext_hi[h, 0:256, :], ext_lo[h, 0:256, :] = parts[0], parts[1]
-
-    prepare(0)
+    wides = [jnp.concatenate([modes[c, :, 128 * h : 128 * (h + 1)] for c in range(3)], axis=1) for h in range(2)]
+    parts = [split3(wide) for wide in wides]
+
+    def prepare(h, directions):
+        for j in directions:
+            outgoing[h, j] = sum(dot(choosers[j], part, 1, 0) for part in parts[h])
+
+    prepare(0, FAR_OUT)
     pl.semaphore_wait(barrier, greeted)
     halo[0].send_far()
+    prepare(0, NEAR_OUT)
     halo[0].send_near()
-    prepare(1)
     gram = sum(dot3(modes[c].T, modes[c], 1, 0) for c in range(3))
     first.begin(gram[0:128, 0:128], gram[128:256, 0:128], gram[128:256, 128:256])
+    prepare(1, FAR_OUT + NEAR_OUT)
+    for h in range(2):
+        table[h, 0:256, :] = wides[h]
+        ext_hi[h, 0:256, :], ext_lo[h, 0:256, :] = parts[h][0], parts[h][1]
 
     conn = connect[...]
     columns = columns_of(conn, 10)
@@ -305,6 +389,7 @@
         place[:, 128 * k : 128 * (k + 1)] = (rows == conn[k : k + 1, :]).astype(BF16)
 
     halo[0].forward()
+    first.second()
     halo[1].send_far()
     halo[1].send_near()
 
@@ -345,6 +430,7 @@
         return carry
 
     lax.fori_loop(0, 16, assemble, 0)
+    first.third()
 
     def multiply(h):
         def group(g, carry):
@@ -377,10 +463,9 @@
     halo[0].receive_far()
     gather(0, 2)
     halves = multiply(0)
-    first.across()
+    halo[1].forward()
     scatter(0, halves, FAR)
     back[0].send_far()
-    halo[1].forward()
     scatter(0, halves, NEAR)
     back[0].send_near()
     scatter(0, halves, OWN)
@@ -388,13 +473,13 @@
     gather(1, 1)
     halo[1].receive_far()
     gather(1, 2)
-    first.gather()
     halves = multiply(1)
+    back[0].forward()
     scatter(1, halves, FAR)
     back[1].send_far()
-    back[0].forward()
     scatter(1, halves, NEAR)
     back[1].send_near()
+    first.fourth()
     scatter(1, halves, OWN)
 
     lower, diagonal = [], 0.0
@@ -434,6 +519,7 @@
     r01 = dot(i00, first.total[128:256, :], 1, 1, HIGH)
     factor_start(work, first.total[256:384, :] - dot(r01, r01, 0, 0, HIGH))
     factor(work, 0)
+    cross.second()
     factor(work, 64)
     r11, i11 = factored(work)
     r_out[0:128, 0:128], r_out[0:128, 128:256] = r00, r01
@@ -441,16 +527,15 @@
     i10 = dot(i11, dot(r01, i00, 0, 0, HIGH), 1, 0, HIGH)
     inv = jnp.concatenate(
         [jnp.concatenate([i00, jnp.zeros((SIDE, SIDE), F32)], axis=1), jnp.concatenate([-i10, i11], axis=1)], axis=0)
-    cross.across()
+    cross.third()
     for c in range(3):
         q_out[c, :, 0:256] = dot3(modes[c], inv, 1, 1) * scale
 
+    cross.fourth()
     complete(1)
     both = sum(dot3(stiff[c, :, 128:256].T, stiff[c], 1, 0) for c in range(3))
     bottom.begin(both[:, 0:128], both[:, 128:256])
-    cross.gather()
     top.across()
-    top.gather()
     cross.end()
     crossed = cross.total
     gram = jnp.concatenate(
@@ -458,19 +543,21 @@
          jnp.concatenate([crossed[128:256, :], crossed[256:384, :]], axis=1)], axis=0)
     low = dot(gram, inv, 1, 1, HIGH)
     low_out[...] = low
+    top.gather()
+    for c in range(3):
+        stiff[c] = stiff[c] - dot3(q_out[c, :, 0:256], low / scale, 1, 1)
+    bottom.across()
     top.end()
     factor_start(work, top.total[...] - dot(low[0:128, :], low[0:128, :], 1, 1, HIGH))
     factor(work, 0)
-    bottom.across()
+    bottom.gather()
     factor(work, 64)
-    bottom.gather()
     r22, i22 = factored(work)
     top_out[...] = r22
     inv_out[...] = i22
     for c in range(3):
-        rest = stiff[c] - dot3(q_out[c, :, 0:256], low / scale, 1, 1)
-        q_out[c, :, 256:384] = dot3(rest[:, 0:128], i22, 1, 1) * scale
-        rest_out[c] = rest[:, 128:256]
+        q_out[c, :, 256:384] = dot3(stiff[c, :, 0:128], i22, 1, 1) * scale
+        rest_out[c] = stiff[c, :, 128:256]
     for h in range(2):
         halo[h].drain()
         back[h].drain()
@@ -506,22 +593,23 @@
             pltpu.VMEM((1280, 384), F32),
             pltpu.VMEM((3, 256, 256), F32),
             pltpu.VMEM((SIDE, 2 * SIDE), F32),
-        ] + sum_scratch(3) + sum_scratch(3) + sum_scratch(1) + sum_scratch(2),
+        ] + blk_sum_scratch() + blk_sum_scratch() + sum_scratch(1) + sum_scratch(2),
         compiler_params=pltpu.CompilerParams(collective_id=1, has_side_effects=True, vmem_limit_bytes=LIMIT),
         name="up_to_last_gram",
     )(count, modes, stiffness, connect, send)
 
 
-def second_kernel(scale, bottom, low, r_first, r_top, i_top, rest, q_in, q_out, r_out, work, top_columns, last, sems):
-    done = pltpu.make_async_copy(q_in, q_out.at[:, :, pl.ds(0, 384)], sems.at[0])
-    fetch = pltpu.make_async_copy(q_in.at[:, :, pl.ds(256, 128)], top_columns, sems.at[1])
-    done.start()
+def second_kernel(scale, bottom, low, r_first, r_top, i_top, rest, q_in, q_out, r_out, work, columns, last, sems):
+    fetch = pltpu.make_async_copy(q_in, columns, sems.at[0])
+    done = pltpu.make_async_copy(columns, q_out.at[:, :, pl.ds(0, 384)], sems.at[1])
     fetch.start()
     low0, low1 = low[0:128, :], low[128:256, :]
     side = bottom[0:128, :] - dot(low1, low0, 1, 1, HIGH)
     r01 = dot(i_top[...], side, 1, 1, HIGH)
     factor_start(work, bottom[128:256, :] - dot(low1, low1, 1, 1, HIGH) - dot(r01, r01, 0, 0, HIGH))
     factor(work, 0)
+    fetch.wait()
+    done.start()
     r_out[0:256, 0:256] = r_first[...] / scale
     r_out[0:256, 256:512] = low[...].T / scale
     r_out[256:512, 0:256] = jnp.zeros((256, 256), F32)
@@ -531,9 +619,8 @@
     factor(work, 64)
     r11, i11 = factored(work)
     r_out[384:512, 384:512] = r11 / scale
-    fetch.wait()
     for c in range(3):
-        left = rest[c] - dot3(top_columns[c], r01 / scale, 1, 0)
+        left = rest[c] - dot3(columns[c, :, 256:384], r01 / scale, 1, 0)
         last[c] = dot3(left, i11, 1, 1) * scale
     place = pltpu.make_async_copy(last, q_out.at[:, :, pl.ds(384, 128)], sems.at[2])
     place.start()
@@ -550,7 +637,7 @@
         out_specs=[anywhere, VMEM],
         scratch_shapes=[
             pltpu.VMEM((SIDE, 2 * SIDE), F32),
-            pltpu.VMEM((3, 256, 128), F32),
+            pltpu.VMEM((3, 256, 384), F32),
             pltpu.VMEM((3, 256, 128), F32),
             pltpu.SemaphoreType.DMA((3,)),
         ],

time: 141 us -> 110 us (0.78)
  Pallas kernels: 139 us -> 108 us
    pallas_call x1, Pallas kernels: 39.1 us -> 8.2 us  [second(): pl.pallas_call(functools.partial(second_kernel, scale), out_shape=[jax.Sh...]
where the time goes in v5:
time: 110 us; the launch traced here: 109 us
  Pallas kernels  108 us (98%)
  between operations  1.47 us (1%)
    pallas_call x1, Pallas kernels, up_to_last_gram(): pl.pallas_call(functools.partial(main_kernel, scale), out_shape=[jax.Shap...  99.7 us
    pallas_call x1, Pallas kernels, second(): pl.pallas_call(functools.partial(second_kernel, scale), out_shape=[jax.Sh...  8.2 us

profile of v5, /device:TPU:0, one launch (start us, length us, event | category | flops | bytes accessed | tf_op | source)
XLA Modules:
  0.0 109.3 jit_solution(2849612326721335187)
XLA Ops:
  1.3 99.7 %up_to_last_gram.1 = (f32[256,128]{1,0:T(8,128)}, f32[256,256]{1,0:T(8,128)}, f32[3,256,128]{2,1,0:T(8,128)}, f32[256,256]{1,0:T(8,128)}, f32[128,128]{1,0:T(8,1...) custom-call(s32[1]{0:T(128)S(6)} %copy.7.count, f32[3,256,256]{2,1,0:T(8,128)} %bitcast.3, ...), custom_call_target="tpu_custom_call" | custom-call | tf_op jit(solution)/shard_map/up_to_last_gram/pallas_call | solution.py:578
  101.0 8.2 %second_factor.1 = (f32[3,256,512]{2,1,0:T(8,128)}, f32[512,512]{1,0:T(8,128)}) custom-call(f32[256,128]{1,0:T(8,128)} %get-tuple-element.11.bottom, f32[256,256]{1,0:T(8,128)} %get-tuple-element.12.low, f32[256,256]{1,0:T(8,128)} %get-tuple-element.13.r_first, f32[128,128]{1,0:T(8,128)} %get-tuple-element.14.r_top, f32[128,128]{1,0:T(8,128)} %get-tuple-element.15.i_top, ...), custom_call_target="tpu_custom_call" | custom-call | tf_op jit(solution)/shard_map/second_factor/pallas_call | solution.py:633

commit v6 on v2

--- a/solution.py
+++ b/solution.py
@@ -141,11 +141,14 @@
         lane = start + 8 * p
         rest = range(p, count)
         col = [{t: jnp.broadcast_to(x[t][0][:, lane + j : lane + j + 1], (8, 128)) for t in rest} for j in range(8)]
+        diagonal = [jnp.broadcast_to(col[k][p][k : k + 1, :], (8, 128)) for k in range(8)]
         for j in range(8):
-            inverse = lax.rsqrt(jnp.broadcast_to(col[j][p][j : j + 1, :], (8, 128)))
+            below = {k: jnp.broadcast_to(col[j][p][k : k + 1, :], (8, 128)) for k in range(j + 1, 8)}
+            inverse = lax.rsqrt(diagonal[j])
             low = {t: col[j][t] * inverse for t in rest}
             for k in range(j + 1, 8):
-                pivot = jnp.broadcast_to(low[p][k : k + 1, :], (8, 128))
+                pivot = below[k] * inverse
+                diagonal[k] = diagonal[k] - pivot * pivot
                 for t in rest:
                     col[k][t] = col[k][t] - low[t] * pivot
             for i in range(tiles):
@@ -243,7 +246,7 @@
 
 def main_kernel(scale, count, modes, stiffness, connect, send, bottom_out, low_out, rest_out, r_out, top_out, inv_out, q_out,
                 outgoing, table, relay, acc, incoming, relay_back, halo_sems, back_sems,
-                ext_hi, ext_lo, pick, place, taken, blocks, matrix_hi, matrix_lo, product, stiff, work, *sums):
+                ext, pick, place, taken, blocks, matrix_hi, matrix_lo, product, stiff, work, *sums):
     leaf, blk = lax.axis_index("leaf"), lax.axis_index("blk")
     device = blk * N_LEAF + leaf
     barrier = greet(leaf, blk)
@@ -276,21 +279,26 @@
     nodes = lax.broadcasted_iota(jnp.int32, (128, 256), 1).astype(F32)
     choosers = [(columns[:, j : j + 1] == nodes).astype(BF16) for j in range(4)]
 
-    def prepare(h):
-        wide = jnp.concatenate([modes[c, :, 128 * h : 128 * (h + 1)] for c in range(3)], axis=1)
-        parts = split3(wide)
-        for j in FAR_OUT + NEAR_OUT:
-            outgoing[h, j] = sum(dot(choosers[j], part, 1, 0) for part in parts)
-        table[h, 0:256, :] = wide
-        ext_hi[h, 0:256, :], ext_lo[h, 0:256, :] = parts[0], parts[1]
-
-    prepare(0)
+    wides = [jnp.concatenate([modes[c, :, 128 * h : 128 * (h + 1)] for c in range(3)], axis=1) for h in range(2)]
+    parts = [split3(wide) for wide in wides]
+    sent = [jnp.concatenate(part, axis=1) for part in parts]
+
+    def prepare(h, directions):
+        for j in directions:
+            found = dot(choosers[j], sent[h], 1, 0)
+            outgoing[h, j] = found[:, 0:384] + (found[:, 384:768] + found[:, 768:1152])
+
+    prepare(0, FAR_OUT)
     pl.semaphore_wait(barrier, greeted)
     halo[0].send_far()
+    prepare(0, NEAR_OUT)
     halo[0].send_near()
-    prepare(1)
     gram = sum(dot3(modes[c].T, modes[c], 1, 0) for c in range(3))
     first.begin(gram[0:128, 0:128], gram[128:256, 0:128], gram[128:256, 128:256])
+    prepare(1, FAR_OUT + NEAR_OUT)
+    for h in range(2):
+        table[h, 0:256, :] = wides[h]
+        ext[h, 0:256, 0:384], ext[h, 0:256, 384:768] = parts[h][0], parts[h][1]
 
     conn = connect[...]
     columns = columns_of(conn, 10)
@@ -311,12 +319,13 @@
     def gather(h, part):
         span = slice(256 * part, 256 * (part + 1))
         if part:
-            ext_hi[h, span, :], ext_lo[h, span, :] = split2(table[h, span, :])
+            ext[h, span, 0:384], ext[h, span, 384:768] = split2(table[h, span, :])
 
         def body(step, carry):
             at = pl.ds(pl.multiple_of(step * 320, 320), 320)
             picked = pick[at, span]
-            found = dot(picked, ext_hi[h, span, :], 1, 0) + dot(picked, ext_lo[h, span, :], 1, 0)
+            found = dot(picked, ext[h, span, :], 1, 0)
+            found = found[:, 0:384] + found[:, 384:768]
             taken[h, at, :] = found if part == 0 else taken[h, at, :] + found
             return carry
 
@@ -356,19 +365,21 @@
             )
             v_hi, v_lo = split2(vectors)
             m_hi, m_lo = matrix_hi[g], matrix_lo[g]
-            result = dot(m_hi, v_hi, 1, 0) + (dot(m_hi, v_lo, 1, 0) + dot(m_lo, v_hi, 1, 0))
+            result = dot(m_hi, jnp.concatenate([v_hi, v_lo], axis=1), 1, 0)
+            result = result[:, 0:128] + (result[:, 128:256] + dot(m_lo, v_hi, 1, 0))
             for c in range(3):
                 for k in range(10):
                     n = 10 * c + k
                     product[spans[k], 128 * c : 128 * (c + 1)] = result[8 * n : 8 * n + 8, :]
             return carry
 
-        lax.fori_loop(0, 16, group, 0, unroll=2)
-        return split2(product[...])
+        lax.fori_loop(0, 16, group, 0, unroll=4)
+        return jnp.concatenate(split2(product[...]), axis=1)
 
     def scatter(h, halves, span):
         where = place[span, :]
-        acc[h, span, :] = dot(where, halves[0], 1, 0) + dot(where, halves[1], 1, 0)
+        found = dot(where, halves, 1, 0)
+        acc[h, span, :] = found[:, 0:384] + found[:, 384:768]
 
     OWN, NEAR, FAR = slice(0, 256), slice(256, 512), slice(512, 768)
 
@@ -377,12 +388,12 @@
     halo[0].receive_far()
     gather(0, 2)
     halves = multiply(0)
-    first.across()
+    halo[1].forward()
     scatter(0, halves, FAR)
     back[0].send_far()
-    halo[1].forward()
     scatter(0, halves, NEAR)
     back[0].send_near()
+    first.across()
     scatter(0, halves, OWN)
     halo[1].receive_near()
     gather(1, 1)
@@ -390,9 +401,9 @@
     gather(1, 2)
     first.gather()
     halves = multiply(1)
+    back[0].forward()
     scatter(1, halves, FAR)
     back[1].send_far()
-    back[0].forward()
     scatter(1, halves, NEAR)
     back[1].send_near()
     scatter(1, halves, OWN)
@@ -400,7 +411,8 @@
     lower, diagonal = [], 0.0
     for c in range(3):
         at = slice(128 * c, 128 * (c + 1))
-        tables = [jnp.concatenate([ext[0, :, at], ext[1, :, at]], axis=1) for ext in (ext_hi, ext_lo)]
+        low_at = slice(384 + 128 * c, 512 + 128 * c)
+        tables = [jnp.concatenate([ext[0, :, lanes], ext[1, :, lanes]], axis=1) for lanes in (at, low_at)]
         for h in range(2):
             hi, lo = split2(acc[h, :, at].T)
             t_hi, t_lo = (t if h else t[:, 0:128] for t in tables)
@@ -419,7 +431,8 @@
         back[h].receive_near()
         back[h].receive_far()
         parts = split2(jnp.concatenate([incoming[h, j] for j in range(4)], axis=0))
-        whole = acc[h, OWN, :] + sum(dot(to_own, part, 1, 0) for part in parts)
+        found = dot(to_own, jnp.concatenate(parts, axis=1), 1, 0)
+        whole = acc[h, OWN, :] + (found[:, 0:384] + found[:, 384:768])
         for c in range(3):
             stiff[c, :, 128 * h : 128 * (h + 1)] = whole[:, 128 * c : 128 * (c + 1)]
 
@@ -445,12 +458,11 @@
     for c in range(3):
         q_out[c, :, 0:256] = dot3(modes[c], inv, 1, 1) * scale
 
+    cross.gather()
     complete(1)
     both = sum(dot3(stiff[c, :, 128:256].T, stiff[c], 1, 0) for c in range(3))
     bottom.begin(both[:, 0:128], both[:, 128:256])
-    cross.gather()
     top.across()
-    top.gather()
     cross.end()
     crossed = cross.total
     gram = jnp.concatenate(
@@ -458,19 +470,21 @@
          jnp.concatenate([crossed[128:256, :], crossed[256:384, :]], axis=1)], axis=0)
     low = dot(gram, inv, 1, 1, HIGH)
     low_out[...] = low
+    top.gather()
+    for c in range(3):
+        stiff[c] = stiff[c] - dot3(q_out[c, :, 0:256], low / scale, 1, 1)
+    bottom.across()
     top.end()
     factor_start(work, top.total[...] - dot(low[0:128, :], low[0:128, :], 1, 1, HIGH))
     factor(work, 0)
-    bottom.across()
+    bottom.gather()
     factor(work, 64)
-    bottom.gather()
     r22, i22 = factored(work)
     top_out[...] = r22
     inv_out[...] = i22
     for c in range(3):
-        rest = stiff[c] - dot3(q_out[c, :, 0:256], low / scale, 1, 1)
-        q_out[c, :, 256:384] = dot3(rest[:, 0:128], i22, 1, 1) * scale
-        rest_out[c] = rest[:, 128:256]
+        q_out[c, :, 256:384] = dot3(stiff[c, :, 0:128], i22, 1, 1) * scale
+        rest_out[c] = stiff[c, :, 128:256]
     for h in range(2):
         halo[h].drain()
         back[h].drain()
@@ -495,8 +509,7 @@
         out_specs=[VMEM] * len(shapes),
         scratch_shapes=[
             rows, table, relay, table, rows, relay, sems, sems,
-            pltpu.VMEM((2, 768, 384), BF16),
-            pltpu.VMEM((2, 768, 384), BF16),
+            pltpu.VMEM((2, 768, 768), BF16),
             pltpu.VMEM((1280, 768), BF16),
             pltpu.VMEM((768, 1280), BF16),
             pltpu.VMEM((2, 1280, 384), F32),
@@ -512,16 +525,17 @@
     )(count, modes, stiffness, connect, send)
 
 
-def second_kernel(scale, bottom, low, r_first, r_top, i_top, rest, q_in, q_out, r_out, work, top_columns, last, sems):
-    done = pltpu.make_async_copy(q_in, q_out.at[:, :, pl.ds(0, 384)], sems.at[0])
-    fetch = pltpu.make_async_copy(q_in.at[:, :, pl.ds(256, 128)], top_columns, sems.at[1])
-    done.start()
+def second_kernel(scale, bottom, low, r_first, r_top, i_top, rest, q_in, q_out, r_out, work, columns, last, sems):
+    fetch = pltpu.make_async_copy(q_in, columns, sems.at[0])
+    done = pltpu.make_async_copy(columns, q_out.at[:, :, pl.ds(0, 384)], sems.at[1])
     fetch.start()
     low0, low1 = low[0:128, :], low[128:256, :]
     side = bottom[0:128, :] - dot(low1, low0, 1, 1, HIGH)
     r01 = dot(i_top[...], side, 1, 1, HIGH)
     factor_start(work, bottom[128:256, :] - dot(low1, low1, 1, 1, HIGH) - dot(r01, r01, 0, 0, HIGH))
     factor(work, 0)
+    fetch.wait()
+    done.start()
     r_out[0:256, 0:256] = r_first[...] / scale
     r_out[0:256, 256:512] = low[...].T / scale
     r_out[256:512, 0:256] = jnp.zeros((256, 256), F32)
@@ -531,9 +545,8 @@
     factor(work, 64)
     r11, i11 = factored(work)
     r_out[384:512, 384:512] = r11 / scale
-    fetch.wait()
     for c in range(3):
-        left = rest[c] - dot3(top_columns[c], r01 / scale, 1, 0)
+        left = rest[c] - dot3(columns[c, :, 256:384], r01 / scale, 1, 0)
         last[c] = dot3(left, i11, 1, 1) * scale
     place = pltpu.make_async_copy(last, q_out.at[:, :, pl.ds(384, 128)], sems.at[2])
     place.start()
@@ -550,7 +563,7 @@
         out_specs=[anywhere, VMEM],
         scratch_shapes=[
             pltpu.VMEM((SIDE, 2 * SIDE), F32),
-            pltpu.VMEM((3, 256, 128), F32),
+            pltpu.VMEM((3, 256, 384), F32),
             pltpu.VMEM((3, 256, 128), F32),
             pltpu.SemaphoreType.DMA((3,)),
         ],

time: 141 us -> 111 us (0.79)
  Pallas kernels: 139 us -> 110 us
    pallas_call x1, Pallas kernels: 39.1 us -> 9.18 us  [second(): pl.pallas_call(functools.partial(second_kernel, scale), out_shape=[jax.Sh...]
where the time goes in v6:
time: 111 us
  Pallas kernels  110 us (99%)
  between operations  1.47 us (1%)
    pallas_call x1, Pallas kernels, up_to_last_gram(): pl.pallas_call(functools.partial(main_kernel, scale), out_shape=[jax.Shap...  100 us
    pallas_call x1, Pallas kernels, second(): pl.pallas_call(functools.partial(second_kernel, scale), out_shape=[jax.Sh...  9.18 us

profile of v6, /device:TPU:0, one launch (start us, length us, event | category | flops | bytes accessed | tf_op | source)
XLA Modules:
  0.0 111.1 jit_solution(143906703253781521)
XLA Ops:
  1.3 100.5 %up_to_last_gram.1 = (f32[256,128]{1,0:T(8,128)}, f32[256,256]{1,0:T(8,128)}, f32[3,256,128]{2,1,0:T(8,128)}, f32[256,256]{1,0:T(8,128)}, f32[128,128]{1,0:T(8,1...) custom-call(s32[1]{0:T(128)S(6)} %copy.7.count, f32[3,256,256]{2,1,0:T(8,128)} %bitcast.3, ...), custom_call_target="tpu_custom_call" | custom-call | tf_op jit(solution)/shard_map/up_to_last_gram/pallas_call | solution.py:505
  101.7 9.2 %second_factor.1 = (f32[3,256,512]{2,1,0:T(8,128)}, f32[512,512]{1,0:T(8,128)}) custom-call(f32[256,128]{1,0:T(8,128)} %get-tuple-element.11.bottom, f32[256,256]{1,0:T(8,128)} %get-tuple-element.12.low, f32[256,256]{1,0:T(8,128)} %get-tuple-element.13.r_first, f32[128,128]{1,0:T(8,128)} %get-tuple-element.14.r_top, f32[128,128]{1,0:T(8,128)} %get-tuple-element.15.i_top, ...), custom_call_target="tpu_custom_call" | custom-call | tf_op jit(solution)/shard_map/second_factor/pallas_call | solution.py:559

commit v7 on v6

--- a/solution.py
+++ b/solution.py
@@ -119,7 +119,7 @@
 
 
 SIDE = 128
-BLOCK = 64
+BLOCK = 32
 
 
 def factor_start(work, gram):
@@ -141,14 +141,11 @@
         lane = start + 8 * p
         rest = range(p, count)
         col = [{t: jnp.broadcast_to(x[t][0][:, lane + j : lane + j + 1], (8, 128)) for t in rest} for j in range(8)]
-        diagonal = [jnp.broadcast_to(col[k][p][k : k + 1, :], (8, 128)) for k in range(8)]
         for j in range(8):
-            below = {k: jnp.broadcast_to(col[j][p][k : k + 1, :], (8, 128)) for k in range(j + 1, 8)}
-            inverse = lax.rsqrt(diagonal[j])
+            inverse = lax.rsqrt(jnp.broadcast_to(col[j][p][j : j + 1, :], (8, 128)))
             low = {t: col[j][t] * inverse for t in rest}
             for k in range(j + 1, 8):
-                pivot = below[k] * inverse
-                diagonal[k] = diagonal[k] - pivot * pivot
+                pivot = jnp.broadcast_to(low[p][k : k + 1, :], (8, 128))
                 for t in rest:
                     col[k][t] = col[k][t] - low[t] * pivot
             for i in range(tiles):
@@ -160,6 +157,11 @@
                     x[t][i] = moved
         for i in range(tiles):
             work[start + 8 * p : start + 8 * p + 8, 128 * i : 128 * (i + 1)] = x[p][i]
+
+
+def factor_half(work, half):
+    for start in range(64 * half, 64 * half + 64, BLOCK):
+        factor(work, start)
 
 
 def factored(work):
@@ -438,20 +440,20 @@
 
     first.end()
     factor_start(work, first.total[0:128, :])
-    factor(work, 0)
+    factor_half(work, 0)
     back[1].forward()
-    factor(work, 64)
+    factor_half(work, 1)
     r00, i00 = factored(work)
     complete(0)
     top.begin(sum(dot3(stiff[c, :, 0:128].T, stiff[c, :, 0:128], 1, 0) for c in range(3)))
-    r01 = dot(i00, first.total[128:256, :], 1, 1, HIGH)
+    r01 = dot3(i00, first.total[128:256, :], 1, 1)
     factor_start(work, first.total[256:384, :] - dot(r01, r01, 0, 0, HIGH))
-    factor(work, 0)
-    factor(work, 64)
+    factor_half(work, 0)
+    factor_half(work, 1)
     r11, i11 = factored(work)
     r_out[0:128, 0:128], r_out[0:128, 128:256] = r00, r01
     r_out[128:256, 0:128], r_out[128:256, 128:256] = jnp.zeros((SIDE, SIDE), F32), r11
-    i10 = dot(i11, dot(r01, i00, 0, 0, HIGH), 1, 0, HIGH)
+    i10 = dot3(i11, dot3(r01.T, i00, 1, 0), 1, 0)
     inv = jnp.concatenate(
         [jnp.concatenate([i00, jnp.zeros((SIDE, SIDE), F32)], axis=1), jnp.concatenate([-i10, i11], axis=1)], axis=0)
     cross.across()
@@ -468,7 +470,7 @@
     gram = jnp.concatenate(
         [jnp.concatenate([crossed[0:128, :], crossed[128:256, :].T], axis=1),
          jnp.concatenate([crossed[128:256, :], crossed[256:384, :]], axis=1)], axis=0)
-    low = dot(gram, inv, 1, 1, HIGH)
+    low = dot3(gram, inv, 1, 1)
     low_out[...] = low
     top.gather()
     for c in range(3):
@@ -476,9 +478,9 @@
     bottom.across()
     top.end()
     factor_start(work, top.total[...] - dot(low[0:128, :], low[0:128, :], 1, 1, HIGH))
-    factor(work, 0)
+    factor_half(work, 0)
     bottom.gather()
-    factor(work, 64)
+    factor_half(work, 1)
     r22, i22 = factored(work)
     top_out[...] = r22
     inv_out[...] = i22
@@ -530,10 +532,10 @@
     done = pltpu.make_async_copy(columns, q_out.at[:, :, pl.ds(0, 384)], sems.at[1])
     fetch.start()
     low0, low1 = low[0:128, :], low[128:256, :]
-    side = bottom[0:128, :] - dot(low1, low0, 1, 1, HIGH)
-    r01 = dot(i_top[...], side, 1, 1, HIGH)
+    side = bottom[0:128, :] - dot3(low1, low0, 1, 1)
+    r01 = dot3(i_top[...], side, 1, 1)
     factor_start(work, bottom[128:256, :] - dot(low1, low1, 1, 1, HIGH) - dot(r01, r01, 0, 0, HIGH))
-    factor(work, 0)
+    factor_half(work, 0)
     fetch.wait()
     done.start()
     r_out[0:256, 0:256] = r_first[...] / scale
@@ -542,7 +544,7 @@
     r_out[256:384, 256:384] = r_top[...] / scale
     r_out[256:384, 384:512] = r01 / scale
     r_out[384:512, 256:384] = jnp.zeros((128, 128), F32)
-    factor(work, 64)
+    factor_half(work, 1)
     r11, i11 = factored(work)
     r_out[384:512, 384:512] = r11 / scale
     for c in range(3):

time: 111 us -> 110 us (level)
  no operation moved by 1% of the time
where the time goes in v7:
time: 110 us
  Pallas kernels  109 us (99%)
  between operations  1.47 us (1%)
    pallas_call x1, Pallas kernels, up_to_last_gram(): pl.pallas_call(functools.partial(main_kernel, scale), out_shape=[jax.Shap...  101 us
    pallas_call x1, Pallas kernels, second(): pl.pallas_call(functools.partial(second_kernel, scale), out_shape=[jax.Sh...  8.12 us

profile of v7, /device:TPU:0, one launch (start us, length us, event | category | flops | bytes accessed | tf_op | source)
XLA Modules:
  0.0 110.3 jit_solution(5898646428701725167)
XLA Ops:
  1.3 100.7 %up_to_last_gram.1 = (f32[256,128]{1,0:T(8,128)}, f32[256,256]{1,0:T(8,128)}, f32[3,256,128]{2,1,0:T(8,128)}, f32[256,256]{1,0:T(8,128)}, f32[128,128]{1,0:T(8,1...) custom-call(s32[1]{0:T(128)S(6)} %copy.7.count, f32[3,256,256]{2,1,0:T(8,128)} %bitcast.3, ...), custom_call_target="tpu_custom_call" | custom-call | tf_op jit(solution)/shard_map/up_to_last_gram/pallas_call | solution.py:507
  102.0 8.1 %second_factor.1 = (f32[3,256,512]{2,1,0:T(8,128)}, f32[512,512]{1,0:T(8,128)}) custom-call(f32[256,128]{1,0:T(8,128)} %get-tuple-element.11.bottom, f32[256,256]{1,0:T(8,128)} %get-tuple-element.12.low, f32[256,256]{1,0:T(8,128)} %get-tuple-element.13.r_first, f32[128,128]{1,0:T(8,128)} %get-tuple-element.14.r_top, f32[128,128]{1,0:T(8,128)} %get-tuple-element.15.i_top, ...), custom_call_target="tpu_custom_call" | custom-call | tf_op jit(solution)/shard_map/second_factor/pallas_call | solution.py:561

commit v8 on v7

--- a/solution.py
+++ b/solution.py
@@ -457,14 +457,15 @@
     inv = jnp.concatenate(
         [jnp.concatenate([i00, jnp.zeros((SIDE, SIDE), F32)], axis=1), jnp.concatenate([-i10, i11], axis=1)], axis=0)
     cross.across()
+    top.across()
     for c in range(3):
         q_out[c, :, 0:256] = dot3(modes[c], inv, 1, 1) * scale
 
     cross.gather()
+    top.gather()
     complete(1)
     both = sum(dot3(stiff[c, :, 128:256].T, stiff[c], 1, 0) for c in range(3))
     bottom.begin(both[:, 0:128], both[:, 128:256])
-    top.across()
     cross.end()
     crossed = cross.total
     gram = jnp.concatenate(
@@ -472,15 +473,14 @@
          jnp.concatenate([crossed[128:256, :], crossed[256:384, :]], axis=1)], axis=0)
     low = dot3(gram, inv, 1, 1)
     low_out[...] = low
-    top.gather()
-    for c in range(3):
-        stiff[c] = stiff[c] - dot3(q_out[c, :, 0:256], low / scale, 1, 1)
-    bottom.across()
     top.end()
     factor_start(work, top.total[...] - dot(low[0:128, :], low[0:128, :], 1, 1, HIGH))
     factor_half(work, 0)
+    bottom.across()
+    for c in range(3):
+        stiff[c] = stiff[c] - dot3(q_out[c, :, 0:256], low / scale, 1, 1)
+    factor_half(work, 1)
     bottom.gather()
-    factor_half(work, 1)
     r22, i22 = factored(work)
     top_out[...] = r22
     inv_out[...] = i22

time: 110 us -> 110 us (level)
  no operation moved by 1% of the time
where the time goes in v8:
time: 110 us
  Pallas kernels  109 us (99%)
  between operations  1.47 us (1%)
    pallas_call x1, Pallas kernels, up_to_last_gram(): pl.pallas_call(functools.partial(main_kernel, scale), out_shape=[jax.Shap...  100 us
    pallas_call x1, Pallas kernels, second(): pl.pallas_call(functools.partial(second_kernel, scale), out_shape=[jax.Sh...  8.12 us

profile of v8, /device:TPU:0, one launch (start us, length us, event | category | flops | bytes accessed | tf_op | source)
XLA Modules:
  0.0 110.0 jit_solution(12256911010011446579)
XLA Ops:
  1.3 100.4 %up_to_last_gram.1 = (f32[256,128]{1,0:T(8,128)}, f32[256,256]{1,0:T(8,128)}, f32[3,256,128]{2,1,0:T(8,128)}, f32[256,256]{1,0:T(8,128)}, f32[128,128]{1,0:T(8,1...) custom-call(s32[1]{0:T(128)S(6)} %copy.7.count, f32[3,256,256]{2,1,0:T(8,128)} %bitcast.3, ...), custom_call_target="tpu_custom_call" | custom-call | tf_op jit(solution)/shard_map/up_to_last_gram/pallas_call | solution.py:507
  101.7 8.1 %second_factor.1 = (f32[3,256,512]{2,1,0:T(8,128)}, f32[512,512]{1,0:T(8,128)}) custom-call(f32[256,128]{1,0:T(8,128)} %get-tuple-element.11.bottom, f32[256,256]{1,0:T(8,128)} %get-tuple-element.12.low, f32[256,256]{1,0:T(8,128)} %get-tuple-element.13.r_first, f32[128,128]{1,0:T(8,128)} %get-tuple-element.14.r_top, f32[128,128]{1,0:T(8,128)} %get-tuple-element.15.i_top, ...), custom_call_target="tpu_custom_call" | custom-call | tf_op jit(solution)/shard_map/second_factor/pallas_call | solution.py:561
